TPU v7x, 32 devices: a whole 2x2x4 slice. The times are simulated.
32 devices in a mesh: dp: 16 (over z, y, x), mp: 2 (over core).
Axes of the slice: x: 2, y: 2, z: 4, core: 2. Of those that a mesh axis runs over, the one named last changes fastest.
Arguments:
- hidden_in: float32 [16, 128, 768], P('dp'), may hold values from -6 to 6
- lengths: int32 [16], P('dp'), may hold values from 1 to 128, as said below
- cotangent: float32 [16, 128, 768], P('dp'), may hold values from -6 to 6
- qkv_weight: bfloat16 [1, 768, 3, 768], P(None, 'dp', None, 'mp'), may hold values from -0.21875 to 0.21875
- qv_bias: bfloat16 [1, 2, 768], P(None, None, ('mp', 'dp')), may hold values from -3 to 3
- out_weight: bfloat16 [1, 768, 768], P(None, 'mp', 'dp'), may hold values from -0.875 to 0.875
- out_bias: bfloat16 [1, 768], P(None, 'dp'), may hold values from -3 to 3
- attn_gain: bfloat16 [1, 768], P(None, 'dp'), may hold values from 0.5 to 1.5
- attn_shift: bfloat16 [1, 768], P(None, 'dp'), may hold values from -3 to 3
- up_weight: bfloat16 [1, 768, 3072], P(None, 'dp', 'mp'), may hold values from -0.21875 to 0.21875
- up_bias: bfloat16 [1, 3072], P(None, ('mp', 'dp')), may hold values from -3 to 3
- down_weight: bfloat16 [1, 3072, 768], P(None, 'mp', 'dp'), may hold values from -0.109375 to 0.109375
- down_bias: bfloat16 [1, 768], P(None, 'dp'), may hold values from -3 to 3
- ffn_gain: bfloat16 [1, 768], P(None, 'dp'), may hold values from 0.5 to 1.5
- ffn_shift: bfloat16 [1, 768], P(None, 'dp'), may hold values from -3 to 3
Outputs:
- hidden_out: float32 [16, 128, 768], P('dp')
- grad_input: float32 [16, 128, 768], P('dp')
- grad_qkv_weight: float32 [1, 768, 3, 768], P(None, 'dp', None, 'mp')
- grad_qv_bias: float32 [1, 2, 768], P(None, None, ('mp', 'dp'))
- grad_out_weight: float32 [1, 768, 768], P(None, 'mp', 'dp')
- grad_out_bias: float32 [1, 768], P(None, 'dp')
- grad_attn_gain: float32 [1, 768], P(None, 'dp')
- grad_attn_shift: float32 [1, 768], P(None, 'dp')
- grad_up_weight: float32 [1, 768, 3072], P(None, 'dp', 'mp')
- grad_up_bias: float32 [1, 3072], P(None, ('mp', 'dp'))
- grad_down_weight: float32 [1, 3072, 768], P(None, 'mp', 'dp')
- grad_down_bias: float32 [1, 768], P(None, 'dp')
- grad_ffn_gain: float32 [1, 768], P(None, 'dp')
- grad_ffn_shift: float32 [1, 768], P(None, 'dp')
Inputs may be any that keep to these rules, and one draw needn't show every extreme that they name: `lengths`: each sequence holds 1 to 128 tokens in its first slots, and some sequence holds exactly 128.
All inputs are finite; a program needn't handle non-finite values.
Results may differ from a plain program's by a relative error of at most 0.012.
The roundings to bfloat16 on the way count: a program that leaves them out, or rounds other values in their place, can miss the bound.
Values may be sent and summed in bfloat16 or wider, within the bound.
A program may use at most 128 MiB of HBM per device.

v0:
```python
import math

import jax
import jax.numpy as jnp
from jax import lax
from jax.sharding import PartitionSpec as P

HEAD_DIM = 64


NORM_EPS = 1e-06
MASKED = -1e30


def normalize(residue, gain_vec, shift_vec):
    centre = residue - jnp.mean(residue, axis=-1, keepdims=True)
    inverse = lax.rsqrt(jnp.mean(centre * centre, axis=-1, keepdims=True) + NORM_EPS)
    scaled = centre * inverse
    return (scaled * gain_vec + shift_vec, scaled, inverse)


def normalize_back(upstream, scaled, inverse, gain_vec):
    through = upstream * gain_vec
    d_residue = inverse * (
        through
        - jnp.mean(through, axis=-1, keepdims=True)
        - scaled * jnp.mean(through * scaled, axis=-1, keepdims=True)
    )
    return (d_residue, jnp.sum(upstream * scaled, axis=0), jnp.sum(upstream, axis=0))


def gelu_exact(pre_act):
    return pre_act * 0.5 * (1.0 + lax.erf(pre_act * (1.0 / math.sqrt(2.0))))


def gelu_slope(pre_act):
    normal_cdf = 0.5 * (1.0 + lax.erf(pre_act * (1.0 / math.sqrt(2.0))))
    density = jnp.exp(-0.5 * pre_act * pre_act) * (1.0 / math.sqrt(2.0 * math.pi))
    return normal_cdf + pre_act * density


def attend_scores(queries, keys_b, keymask):
    raw = jnp.einsum("bqhe,bkhe->bhqk", queries, keys_b, preferred_element_type=jnp.float32) * 0.125
    return jnp.where(keymask[:, None, None, :], raw, MASKED)


def my_rows(full_rows):
    half_rows = full_rows.shape[0] // lax.axis_size("mp")
    return lax.dynamic_slice_in_dim(full_rows, lax.axis_index("mp") * half_rows, half_rows, 0)


def forward_rows(half_b):
    return lax.all_gather(half_b, "mp", axis=0, tiled=True)


def forward_sums(partial_value):
    return lax.psum_scatter(partial_value, "mp", scatter_dimension=0, tiled=True)


def backward_rows(half_b):
    return lax.all_gather(half_b, "mp", axis=0, tiled=True)


def backward_sums(partial_value):
    return lax.psum_scatter(partial_value, "mp", scatter_dimension=0, tiled=True)


def fetch_layer(picked):
    return (
        lax.all_gather(picked[0], "dp", axis=0, tiled=True),
        lax.all_gather(picked[1], "dp", axis=1, tiled=True),
        lax.all_gather(picked[2], "dp", axis=1, tiled=True),
        lax.all_gather(picked[3], "dp", axis=0, tiled=True),
        lax.all_gather(picked[4], "dp", axis=0, tiled=True),
        lax.all_gather(picked[5], "dp", axis=0, tiled=True),
        lax.all_gather(picked[6], "dp", axis=0, tiled=True),
        lax.all_gather(picked[7], "dp", axis=0, tiled=True),
        lax.all_gather(picked[8], "dp", axis=1, tiled=True),
        lax.all_gather(picked[9], "dp", axis=0, tiled=True),
        lax.all_gather(picked[10], "dp", axis=0, tiled=True),
        lax.all_gather(picked[11], "dp", axis=0, tiled=True),
    )


def fetch_again(picked):
    return (
        lax.all_gather(picked[0], "dp", axis=0, tiled=True),
        lax.all_gather(picked[1], "dp", axis=1, tiled=True),
        lax.all_gather(picked[2], "dp", axis=1, tiled=True),
        lax.all_gather(picked[3], "dp", axis=0, tiled=True),
        lax.all_gather(picked[4], "dp", axis=0, tiled=True),
        lax.all_gather(picked[5], "dp", axis=0, tiled=True),
        lax.all_gather(picked[6], "dp", axis=0, tiled=True),
        lax.all_gather(picked[7], "dp", axis=0, tiled=True),
        lax.all_gather(picked[8], "dp", axis=1, tiled=True),
        lax.all_gather(picked[9], "dp", axis=0, tiled=True),
        lax.all_gather(picked[10], "dp", axis=0, tiled=True),
        lax.all_gather(picked[11], "dp", axis=0, tiled=True),
    )


def scatter_layer(grads):
    return (
        lax.psum_scatter(grads[0], "dp", scatter_dimension=0, tiled=True),
        lax.psum_scatter(grads[1], "dp", scatter_dimension=1, tiled=True),
        lax.psum_scatter(grads[2], "dp", scatter_dimension=1, tiled=True),
        lax.psum_scatter(grads[3], "dp", scatter_dimension=0, tiled=True),
        lax.psum_scatter(grads[4], "dp", scatter_dimension=0, tiled=True),
        lax.psum_scatter(grads[5], "dp", scatter_dimension=0, tiled=True),
        lax.psum_scatter(grads[6], "dp", scatter_dimension=0, tiled=True),
        lax.psum_scatter(grads[7], "dp", scatter_dimension=0, tiled=True),
        lax.psum_scatter(grads[8], "dp", scatter_dimension=1, tiled=True),
        lax.psum_scatter(grads[9], "dp", scatter_dimension=0, tiled=True),
        lax.psum_scatter(grads[10], "dp", scatter_dimension=0, tiled=True),
        lax.psum_scatter(grads[11], "dp", scatter_dimension=0, tiled=True),
    )


def layer_forward(hidden_half, inputs_b, params, keymask):
    qkv_w, qv_b, out_w, out_b, gain_a, shift_a, up_w, up_b, down_w, down_b, gain_f, shift_f = params
    seq_count, seq_span = keymask.shape
    feat_width = inputs_b.shape[1]
    local_width = qkv_w.shape[2]
    heads_here = local_width // HEAD_DIM
    projected = jnp.dot(
        inputs_b, qkv_w.reshape(feat_width, 3 * local_width), preferred_element_type=jnp.float32
    )
    projected = projected.reshape(seq_count, seq_span, 3, heads_here, HEAD_DIM)
    biases = qv_b.astype(jnp.float32).reshape(2, heads_here, HEAD_DIM)
    queries = (projected[:, :, 0] + biases[0]).astype(jnp.bfloat16)
    keys_b = projected[:, :, 1].astype(jnp.bfloat16)
    values = (projected[:, :, 2] + biases[1]).astype(jnp.bfloat16)
    scores = attend_scores(queries, keys_b, keymask)
    row_peak = jnp.max(scores, axis=-1, keepdims=True)
    logsum = row_peak + jnp.log(jnp.sum(jnp.exp(scores - row_peak), axis=-1, keepdims=True))
    probs_b = jnp.exp(scores - logsum).astype(jnp.bfloat16)
    context = jnp.einsum("bhqk,bkhe->bqhe", probs_b, values, preferred_element_type=jnp.float32)
    context = context.astype(jnp.bfloat16).reshape(seq_count * seq_span, local_width)
    attn_part = jnp.dot(context, out_w, preferred_element_type=jnp.float32)
    attended = forward_sums(attn_part) + out_b.astype(jnp.float32)
    mid_half, scaled_a, inverse_a = normalize(
        hidden_half + attended, gain_a.astype(jnp.float32), shift_a.astype(jnp.float32)
    )
    mid_b = forward_rows(mid_half.astype(jnp.bfloat16))
    pre_act = jnp.dot(mid_b, up_w, preferred_element_type=jnp.float32) + up_b.astype(jnp.float32)
    act_b = gelu_exact(pre_act).astype(jnp.bfloat16)
    mlp_part = jnp.dot(act_b, down_w, preferred_element_type=jnp.float32)
    mlp_out = forward_sums(mlp_part) + down_b.astype(jnp.float32)
    output, scaled_f, inverse_f = normalize(
        mid_half + mlp_out, gain_f.astype(jnp.float32), shift_f.astype(jnp.float32)
    )
    return (
        output,
        (
            inputs_b,
            queries,
            keys_b,
            values,
            logsum,
            context,
            scaled_a,
            inverse_a,
            mid_b,
            pre_act,
            act_b,
            scaled_f,
            inverse_f,
        ),
    )


def layer_backward(upstream_half, params, kept_state, keymask):
    qkv_w, qv_b, out_w, out_b, gain_a, shift_a, up_w, up_b, down_w, down_b, gain_f, shift_f = params
    (
        inputs_b,
        queries,
        keys_b,
        values,
        logsum,
        context,
        scaled_a,
        inverse_a,
        mid_b,
        pre_act,
        act_b,
        scaled_f,
        inverse_f,
    ) = kept_state
    seq_count, seq_span = keymask.shape
    feat_width = inputs_b.shape[1]
    local_width = qkv_w.shape[2]
    heads_here = local_width // HEAD_DIM
    d_resid_f, part_gain_f, part_shift_f = normalize_back(
        upstream_half, scaled_f, inverse_f, gain_f.astype(jnp.float32)
    )
    part_down_b = jnp.sum(d_resid_f, axis=0)
    mlp_b = backward_rows(d_resid_f.astype(jnp.bfloat16))
    grad_down = jnp.dot(act_b.T, mlp_b, preferred_element_type=jnp.float32)
    d_pre = jnp.dot(mlp_b, down_w.T, preferred_element_type=jnp.float32) * gelu_slope(pre_act)
    d_pre_b = d_pre.astype(jnp.bfloat16)
    grad_up = jnp.dot(mid_b.T, d_pre_b, preferred_element_type=jnp.float32)
    grad_up_b = jnp.sum(d_pre, axis=0)
    mid_part = jnp.dot(d_pre_b, up_w.T, preferred_element_type=jnp.float32)
    d_mid = d_resid_f + backward_sums(mid_part)
    d_resid_a, part_gain_a, part_shift_a = normalize_back(
        d_mid, scaled_a, inverse_a, gain_a.astype(jnp.float32)
    )
    part_out_b = jnp.sum(d_resid_a, axis=0)
    attn_b = backward_rows(d_resid_a.astype(jnp.bfloat16))
    grad_out = jnp.dot(context.T, attn_b, preferred_element_type=jnp.float32)
    d_context = jnp.dot(attn_b, out_w.T, preferred_element_type=jnp.float32).astype(jnp.bfloat16)
    d_context = d_context.reshape(seq_count, seq_span, heads_here, HEAD_DIM)
    scores = attend_scores(queries, keys_b, keymask)
    probs_f = jnp.exp(scores - logsum)
    probs_b = probs_f.astype(jnp.bfloat16)
    d_probs = jnp.einsum("bqhe,bkhe->bhqk", d_context, values, preferred_element_type=jnp.float32)
    d_values = jnp.einsum("bhqk,bqhe->bkhe", probs_b, d_context, preferred_element_type=jnp.float32)
    centred = jnp.sum(probs_f * d_probs, axis=-1, keepdims=True)
    d_scores = (probs_f * (d_probs - centred) * 0.125).astype(jnp.bfloat16)
    d_queries = jnp.einsum("bhqk,bkhe->bqhe", d_scores, keys_b, preferred_element_type=jnp.float32)
    d_keys = jnp.einsum("bhqk,bqhe->bkhe", d_scores, queries, preferred_element_type=jnp.float32)
    grad_qv = jnp.stack(
        [jnp.sum(d_queries, axis=(0, 1)).reshape(-1), jnp.sum(d_values, axis=(0, 1)).reshape(-1)]
    )
    d_proj = (
        jnp.stack([d_queries, d_keys, d_values], axis=2)
        .astype(jnp.bfloat16)
        .reshape(seq_count * seq_span, 3 * local_width)
    )
    grad_qkv = jnp.dot(inputs_b.T, d_proj, preferred_element_type=jnp.float32).reshape(
        feat_width, 3, local_width
    )
    input_part = jnp.dot(
        d_proj, qkv_w.reshape(feat_width, 3 * local_width).T, preferred_element_type=jnp.float32
    )
    d_hidden = d_resid_a + backward_sums(input_part)
    grad_gain_a, grad_shift_a, grad_out_b, grad_gain_f, grad_shift_f, grad_down_b = lax.psum(
        (part_gain_a, part_shift_a, part_out_b, part_gain_f, part_shift_f, part_down_b), "mp"
    )
    return (
        d_hidden,
        (
            grad_qkv,
            grad_qv,
            grad_out,
            grad_out_b,
            grad_gain_a,
            grad_shift_a,
            grad_up,
            grad_up_b,
            grad_down,
            grad_down_b,
            grad_gain_f,
            grad_shift_f,
        ),
    )


def body(
    hidden_in,
    lengths,
    cotangent,
    qkv_weight,
    qv_bias,
    out_weight,
    out_bias,
    attn_gain,
    attn_shift,
    up_weight,
    up_bias,
    down_weight,
    down_bias,
    ffn_gain,
    ffn_shift,
):
    seq_count, seq_span, feat_width = hidden_in.shape
    layers_count = qkv_weight.shape[0]
    shards = (
        qkv_weight,
        qv_bias,
        out_weight,
        out_bias,
        attn_gain,
        attn_shift,
        up_weight,
        up_bias,
        down_weight,
        down_bias,
        ffn_gain,
        ffn_shift,
    )
    keymask = jnp.arange(seq_span)[None, :] < lengths[:, None]
    rowmask = keymask.astype(jnp.float32).reshape(-1, 1)
    full_in = hidden_in.reshape(-1, feat_width)
    hidden_half = my_rows(full_in)
    inputs_b = full_in.astype(jnp.bfloat16)
    gathered = []
    layer_at = 0
    params = fetch_layer(tuple((member[layer_at] for member in shards)))
    hidden_half, kept_state = layer_forward(hidden_half, inputs_b, params, keymask)
    gathered.append(params)
    kept_list = [kept_state]
    whole_out = lax.all_gather(hidden_half, "mp", axis=0, tiled=True)
    hidden_out = (whole_out * rowmask).reshape(seq_count, seq_span, feat_width)
    upstream = my_rows(cotangent.reshape(-1, feat_width)) * my_rows(rowmask)
    grads_list = [None] * layers_count
    for layer_at in reversed(range(layers_count)):
        params = fetch_again(tuple((member[layer_at] for member in shards)))
        upstream, layer_grads = layer_backward(upstream, params, kept_list[layer_at], keymask)
        grads_list[layer_at] = scatter_layer(layer_grads)
    stacked = tuple((jnp.stack([grads_list[0][member_at]]) for member_at in range(12)))
    grad_input = lax.all_gather(upstream, "mp", axis=0, tiled=True).reshape(
        seq_count, seq_span, feat_width
    )
    return (
        hidden_out,
        grad_input,
        stacked[0],
        stacked[1],
        stacked[2],
        stacked[3],
        stacked[4],
        stacked[5],
        stacked[6],
        stacked[7],
        stacked[8],
        stacked[9],
        stacked[10],
        stacked[11],
    )


def solution(mesh):
    return jax.shard_map(
        body,
        mesh=mesh,
        in_specs=(
            P("dp", None, None),
            P("dp"),
            P("dp", None, None),
            P(None, "dp", None, "mp"),
            P(None, None, ("mp", "dp")),
            P(None, "mp", "dp"),
            P(None, "dp"),
            P(None, "dp"),
            P(None, "dp"),
            P(None, "dp", "mp"),
            P(None, ("mp", "dp")),
            P(None, "mp", "dp"),
            P(None, "dp"),
            P(None, "dp"),
            P(None, "dp"),
        ),
        out_specs=(
            P("dp", None, None),
            P("dp", None, None),
            P(None, "dp", None, "mp"),
            P(None, None, ("mp", "dp")),
            P(None, "mp", "dp"),
            P(None, "dp"),
            P(None, "dp"),
            P(None, "dp"),
            P(None, "dp", "mp"),
            P(None, ("mp", "dp")),
            P(None, "mp", "dp"),
            P(None, "dp"),
            P(None, "dp"),
            P(None, "dp"),
        ),
        check_vma=False,
    )
```

profile of v0, /device:TPU:0, one launch (start us, length us, event | category | flops | bytes accessed | tf_op | source)
XLA Modules:
  0.0 853.0 jit_solution(8246782652431917449)
XLA Ops:
  8.6 0.8 copy.52
  9.4 43.7 %all-gather.1 = bf16[1,2,384]{1,0,2:T(2,128)(2,1)S(1)} all-gather(bf16[1,2,24]{1,0,2:T(2,128)(2,1)S(1)} %copy.52), channel_id=3, replica_groups=mesh['dp'=16,'mp'=2] {'dp'}, dimensions={2}, use_global_device_ids=true | all-gather | bytes 1632 | tf_op jit(solution)/shard_map/all_gather | solution.py:71
  53.3 1.7 slice_reduce_fusion.1
  55.2 41.0 %all-gather.2 = bf16[1,384,768]{1,2,0:T(8,128)(2,1)S(1)} all-gather(bf16[1,384,48]{1,2,0:T(8,128)(2,1)} %param.20), channel_id=4, replica_groups=mesh['dp'=16,'mp'=2] {'dp'}, dimensions={2}, use_global_device_ids=true | all-gather | bytes 626688 | tf_op jit(solution)/shard_map/all_gather | solution.py:72
  96.2 2.8 copy.51
  101.4 1.1 fusion.22
  107.5 73.8 %all-reduce.17 = (bf16[768]{0:T(1024)(128)(2,1)S(1)}, bf16[768]{0:T(1024)(128)(2,1)S(1)}, bf16[768]{0:T(1024)(128)(2,1)S(1)}, bf16[1536]{0:T(1024)(128)(2,1)S(1)...) all-reduce(bf16[768]{0:T(1024)(128)(2,1)S(1)} %dynamic-update-slice, ...), channel_id=5, replica_groups=mesh['dp'=16,'mp'=2] {'dp'}, use_global_device_ids=true, to_apply=%add | all-reduce | flops 6144 | bytes 24576
  181.3 1.1 fusion.65
  182.7 1.9 all_gather.63
  184.6 2.2 convolution_add_fusion
  186.9 52.0 %all-gather.20.cloned.1.call-done = bf16[1,1536,768]{1,2,0:T(8,128)(2,1)} async-done(((bf16[1,1536,48]{1,2,0:T(8,128)(2,1)}), bf16[1,1536,768]{1,2,0:T(8,128)(2,1)}) %all-gather.20.cloned.1.call-update) | async-done | bytes 2359312 | tf_op jit(solution)/shard_map/all_gather | solution.py:78
  238.9 3.3 fusion.2
  242.4 6.6 reduce-scatter.12.cloned.1.call-done
  249.0 1.3 fusion.64
  250.5 1.7 multiply_reduce_fusion.1
  252.2 2.3 fusion.62
  255.2 2.1 all_gather.71
  257.3 1.3 fusion.70
  258.6 0.7 copy-done.15
  259.3 1.6 fusion.4
  261.0 9.1 %reduce-scatter.14.cloned.1.call-done = f32[64,768]{1,0:T(8,128)} async-done(((f32[128,768]{1,0:T(8,128)}), f32[64,768]{1,0:T(8,128)}) %reduce-scatter.14.cloned.1.call-update) | async-done | bytes 196624 | tf_op jit(solution)/shard_map/reduce_scatter | solution.py:65
  270.1 1.8 multiply_reduce_fusion.2
  271.8 1.4 fusion.63
  273.9 1.9 all_gather.72
  275.9 0.9 convolution_convert_fusion
  276.8 1.0 copy.54
  277.8 0.9 convolution_bitcast_fusion.1
  279.4 2.0 fusion.66
  281.4 1.0 pad_maximum_fusion
  283.1 1.2 fusion.75
  284.4 1.4 fusion.76
  286.1 1.7 fusion.30
  287.8 3.0 copy.58
  290.8 1.1 copy-done.2
  292.0 3.0 fusion.61
  295.1 0.8 copy-done.14
  296.1 2.9 fusion.32
  301.2 2.1 all_gather.70
  303.3 0.8 multiply_bitcast_fusion
  304.3 77.1 %all-reduce.15 = (f32[2,384]{1,0:T(2,128)S(1)}, f32[768]{0:T(1024)S(1)}, f32[768]{0:T(1024)S(1)}, f32[768]{0:T(1024)S(1)}, f32[1536]{0:T(1024)S(1)}, /*index=5*/...) all-reduce(f32[2,384]{1,0:T(2,128)S(1)} %pad_maximum_fusion.1, ...), channel_id=19, replica_groups=mesh['dp'=16,'mp'=2] {'dp'}, use_global_device_ids=true, to_apply=%region_18.19.clone | all-reduce | flops 6912 | bytes 55296
  381.9 3.0 all-reduce.16
  386.1 0.9 add.185
  387.1 2.1 all_gather.73
  389.1 34.4 %reduce-scatter.20.cloned.1.call-done = f32[384,48]{0,1:T(8,128)} async-done(((f32[384,768]{0,1:T(8,128)}), f32[384,48]{0,1:T(8,128)}) %reduce-scatter.20.cloned.1.call-update) | async-done | bytes 73744 | tf_op jit(solution)/shard_map/reduce_scatter | solution.py:106
  423.5 138.0 %reduce-scatter.18.cloned.1.call-done = f32[48,3,384]{2,0,1:T(8,128)} async-done(((f32[768,3,384]{2,0,1:T(8,128)}), f32[48,3,384]{2,0,1:T(8,128)}) %reduce-scatter.18.cloned.1.call-update) | async-done | bytes 221200 | tf_op jit(solution)/shard_map/reduce_scatter | solution.py:104
  561.5 141.4 %reduce-scatter.24.cloned.1.call-done = f32[1536,48]{0,1:T(8,128)} async-done(((f32[1536,768]{0,1:T(8,128)}), f32[1536,48]{0,1:T(8,128)}) %reduce-scatter.24.cloned.1.call-update) | async-done | bytes 294928 | tf_op jit(solution)/shard_map/reduce_scatter | solution.py:112
  702.9 142.8 %reduce-scatter.22.cloned.1.call-done = f32[48,1536]{1,0:T(8,128)} async-done(((f32[768,1536]{1,0:T(8,128)}), f32[48,1536]{1,0:T(8,128)}) %reduce-scatter.22.cloned.1.call-update) | async-done | bytes 294928 | tf_op jit(solution)/shard_map/reduce_scatter | solution.py:110
  845.7 0.7 copy.75
  (163 shorter events, 13.0 us)
Async XLA Ops:
  7.2 89.0 %all-gather.16.cloned.1.call-start = ((), (), s32[]{:S(2)}) async-start(), calls=%async_computation.16 | async-start | bytes 1880064 | tf_op jit(solution)/shard_map/all_gather | solution.py:70
  7.9 173.4 %reduce-scatter.10.cloned.1.call-start = ((), (), s32[]{:S(2)}) async-start(), calls=%async_computation.8 | async-start | bytes 589824 | tf_op jit(solution)/shard_map/reduce_scatter | solution.py:57
  53.3 45.8 %copy-start.8 = (f32[1,128,768]{2,1,0:T(8,128)S(1)}, f32[1,128,768]{2,1,0:T(8,128)}, u32[]{:S(2)}) copy-start(f32[1,128,768]{2,1,0:T(8,128)} %param.15) | copy-start | bytes 1179652
  55.2 44.5 %copy-start.27 = (f32[6,64]{1,0:T(8,128)}, f32[6,64]{1,0:T(8,128)S(1)}, u32[]{:S(2)}) copy-start(f32[6,64]{1,0:T(8,128)S(1)} %add.164) | copy-start | bytes 4612
  96.2 4.6 copy-start.3
  99.7 0.8 copy-start.5
  99.7 4.2 copy-start.32
  99.7 6.1 copy-start.33
  99.7 6.3 copy-start.34
  99.7 6.6 copy-start.35
  99.7 6.8 copy-start.36
  99.8 7.0 copy-start.37
  99.8 7.2 copy-start.38
  99.8 7.5 copy-start.39
  102.5 82.1 %all-gather.18.cloned.1.call-start = ((), (), s32[]{:S(2)}) async-start(), calls=%async_computation.17 | async-start | bytes 2506752 | tf_op jit(solution)/shard_map/all_gather | solution.py:76
  103.3 135.6 %all-gather.20.cloned.1.call-start = ((), (), s32[]{:S(2)}) async-start(), calls=%async_computation.18 | async-start | bytes 2506752 | tf_op jit(solution)/shard_map/all_gather | solution.py:78
  103.8 145.1 %reduce-scatter.12.cloned.1.call-start = ((), (), s32[]{:S(2)}) async-start(), calls=%async_computation.9 | async-start | bytes 589824 | tf_op jit(solution)/shard_map/reduce_scatter | solution.py:57
  182.4 66.6 %copy-start.29 = (f32[64]{0:T(128)}, f32[64]{0:T(128)S(1)}, u32[]{:S(2)}) copy-start(f32[64]{0:T(128)S(1)} %broadcast_multiply_fusion.5) | copy-start | bytes 772
  182.6 66.4 %copy-start.31 = (f32[64]{0:T(128)}, f32[64]{0:T(128)S(1)}, u32[]{:S(2)}) copy-start(f32[64]{0:T(128)S(1)} %add_rsqrt_fusion.1) | copy-start | bytes 772
  184.6 57.6 %copy-start.13 = (bf16[128,768]{1,0:T(8,128)(2,1)}, bf16[128,768]{1,0:T(8,128)(2,1)S(1)}, u32[]{:S(2)}) copy-start(bf16[128,768]{1,0:T(8,128)(2,1)S(1)} %all_gather.63) | copy-start | bytes 589828
  186.9 70.4 %copy-start.1 = (f32[128,1536]{1,0:T(8,128)}, f32[128,1536]{1,0:T(8,128)S(1)}, u32[]{:S(2)}) copy-start(f32[128,1536]{1,0:T(8,128)S(1)} %convolution_add_fusion) | copy-start | bytes 2359300
  242.2 27.8 %reduce-scatter.14.cloned.1.call-start = ((), (), s32[]{:S(2)}) async-start(), calls=%async_computation.10 | async-start | bytes 589824 | tf_op jit(solution)/shard_map/reduce_scatter | solution.py:65
  249.0 8.3 copy-start.9
  255.2 4.1 copy-start
  257.3 1.3 copy-start.19
  258.6 0.7 copy-start.15
  259.3 16.5 %copy-start.4 = (bf16[1,384,768]{1,2,0:T(8,128)(2,1)S(1)}, bf16[1,384,768]{1,2,0:T(8,128)(2,1)}, u32[]{:S(2)}) copy-start(bf16[1,384,768]{1,2,0:T(8,128)(2,1)} %copy-done.3) | copy-start | bytes 1769476
  260.9 17.8 %copy-start.6 = (f32[1,128,3,6,64]{1,4,3,2,0:T(8,128)S(1)}, f32[1,128,3,6,64]{1,4,3,2,0:T(8,128)}, u32[]{:S(2)}) copy-start(f32[1,128,3,6,64]{1,4,3,2,0:T(8,128)} %copy-done.5) | copy-start | bytes 1769476
  261.0 125.1 %reduce-scatter.16.cloned.1.call-start = ((), (), s32[]{:S(2)}) async-start(), calls=%async_computation.11 | async-start | bytes 589824 | tf_op jit(solution)/shard_map/reduce_scatter | solution.py:65
  273.2 5.9 copy-start.28
  279.1 5.3 copy-start.18
  282.4 0.7 copy-start.7
  284.3 139.2 %reduce-scatter.20.cloned.1.call-start = ((), (), s32[]{:S(2)}) async-start(), calls=%async_computation.13 | async-start | bytes 1253376 | tf_op jit(solution)/shard_map/reduce_scatter | solution.py:106
  285.8 275.7 %reduce-scatter.18.cloned.1.call-start = ((), (), s32[]{:S(2)}) async-start(), calls=%async_computation.12 | async-start | bytes 3760128 | tf_op jit(solution)/shard_map/reduce_scatter | solution.py:104
  290.7 1.2 copy-start.2
  290.7 1.3 copy-start.20
  290.8 412.1 %reduce-scatter.24.cloned.1.call-start = ((), (), s32[]{:S(2)}) async-start(), calls=%async_computation.15 | async-start | bytes 5013504 | tf_op jit(solution)/shard_map/reduce_scatter | solution.py:112
  295.0 0.9 copy-start.14
  295.0 1.1 copy-start.16
  295.0 550.7 %reduce-scatter.22.cloned.1.call-start = ((), (), s32[]{:S(2)}) async-start(), calls=%async_computation.14 | async-start | bytes 5013504 | tf_op jit(solution)/shard_map/reduce_scatter | solution.py:110
  299.0 2.1 copy-start.21
  299.0 5.2 copy-start.22
  299.0 5.3 copy-start.23
  299.0 5.3 copy-start.24
  299.0 5.3 copy-start.25
  299.0 5.3 copy-start.26
  299.0 5.3 copy-start.30
  299.1 87.0 %copy-start.11 = (f32[64,768]{1,0:T(8,128)S(1)}, f32[64,768]{1,0:T(8,128)}, u32[]{:S(2)}) copy-start(f32[64,768]{1,0:T(8,128)} %copy-done.10) | copy-start | bytes 589828
  (3 other events, 2.0 us)
Sparse Core Ops, SparseCore 0:
  10.7 64.0 all-gather.15
  102.6 5.0 reduce-scatter.9
  110.9 63.5 all-gather.17
  177.6 61.2 all-gather.19
  242.3 6.5 reduce-scatter.11
  261.1 8.9 reduce-scatter.13
  284.5 8.9 reduce-scatter.15
  298.8 124.7 reduce-scatter.19
  429.2 132.2 reduce-scatter.17
  567.1 135.7 reduce-scatter.23
  709.5 136.1 reduce-scatter.21
where the time goes:
time: 854 us; the launch traced here: 853 us
  waiting for transfers between devices  526 us (62%)
  blocking collectives  249 us (29%)
  matrix products  25.5 us (3%)
  local copies, waits for them, and re-layouts  20.3 us (2%)
  between operations  18.4 us (2%)
  other arithmetic  13.2 us (2%)
    unnamed x2, blocking collectives  151 us
    reduce_scatter x1, waiting for transfers between devices, scatter_layer(): lax.psum_scatter(grads[6], 'dp', scatter_dimension=0, tiled=True)  143 us
    reduce_scatter x1, waiting for transfers between devices, scatter_layer(): lax.psum_scatter(grads[8], 'dp', scatter_dimension=1, tiled=True)  141 us
    reduce_scatter x1, waiting for transfers between devices, scatter_layer(): lax.psum_scatter(grads[0], 'dp', scatter_dimension=0, tiled=True)  138 us
    all_gather x1, waiting for transfers between devices, fetch_layer(): lax.all_gather(picked[8], 'dp', axis=1, tiled=True)  52 us
    all_gather x1, blocking collectives, fetch_layer(): lax.all_gather(picked[1], 'dp', axis=1, tiled=True)  43.7 us
    all_gather x1, blocking collectives, fetch_layer(): lax.all_gather(picked[2], 'dp', axis=1, tiled=True)  41 us
    reduce_scatter x1, waiting for transfers between devices, scatter_layer(): lax.psum_scatter(grads[2], 'dp', scatter_dimension=1, tiled=True)  34.4 us
  transfers between devices with their start and end apart: 11, of which 7 were waited for; matrix products, arithmetic and copies ran while one was open for 3% of the time, Pallas kernels for 0%

commit v1 on v0

v1 whole, which is shorter than its diff:
```python
import math

import jax
import jax.numpy as jnp
from jax import lax
from jax.experimental import pallas as pl
from jax.experimental.pallas import tpu as pltpu
from jax.sharding import PartitionSpec as P

HEAD_DIM = 64


NORM_EPS = 1e-06
MASKED = -1e30


def normalize(residue, gain_vec, shift_vec):
    centre = residue - jnp.mean(residue, axis=-1, keepdims=True)
    inverse = lax.rsqrt(jnp.mean(centre * centre, axis=-1, keepdims=True) + NORM_EPS)
    scaled = centre * inverse
    return (scaled * gain_vec + shift_vec, scaled, inverse)


def normalize_back(upstream, scaled, inverse, gain_vec):
    through = upstream * gain_vec
    d_residue = inverse * (
        through
        - jnp.mean(through, axis=-1, keepdims=True)
        - scaled * jnp.mean(through * scaled, axis=-1, keepdims=True)
    )
    return (d_residue, jnp.sum(upstream * scaled, axis=0), jnp.sum(upstream, axis=0))


def gelu_exact(pre_act):
    return pre_act * 0.5 * (1.0 + lax.erf(pre_act * (1.0 / math.sqrt(2.0))))


def gelu_slope(pre_act):
    normal_cdf = 0.5 * (1.0 + lax.erf(pre_act * (1.0 / math.sqrt(2.0))))
    density = jnp.exp(-0.5 * pre_act * pre_act) * (1.0 / math.sqrt(2.0 * math.pi))
    return normal_cdf + pre_act * density


def attend_scores(queries, keys_b, keymask):
    raw = jnp.einsum("bqhe,bkhe->bhqk", queries, keys_b, preferred_element_type=jnp.float32) * 0.125
    return jnp.where(keymask[:, None, None, :], raw, MASKED)


MESH = pl.DeviceIdType.MESH
BF16 = jnp.bfloat16
F32 = jnp.float32
VMEM_LIMIT = 56 * 1024 * 1024

LINE = 4
SPAN = 16

LAST_TWO = (True, True, False, False, False)


def place_of(me):
    return me // 4, (me // 2) % 2, me % 2


def block_of(place, last, other, last_two):
    return place * 4 + (other * 2 + last if last_two else last * 2 + other)


def greet(me, place, one, two):
    barrier = pltpu.get_barrier_semaphore()
    for partner in (me + 1 - 2 * two, me + 2 - 4 * one):
        pl.semaphore_signal(barrier, inc=1, device_id={"dp": partner}, device_id_type=MESH)

    @pl.when(place > 0)
    def _():
        pl.semaphore_signal(barrier, inc=1, device_id={"dp": me - 4}, device_id_type=MESH)

    @pl.when(place < LINE - 1)
    def _():
        pl.semaphore_signal(barrier, inc=1, device_id={"dp": me + 4}, device_id_type=MESH)

    at_end = (place == 0) | (place == LINE - 1)

    @pl.when(at_end)
    def _():
        pl.semaphore_wait(barrier, 3)

    @pl.when(jnp.logical_not(at_end))
    def _():
        pl.semaphore_wait(barrier, 4)


def gather_kernel(*refs):
    count = len(LAST_TWO)
    mine, full = refs[:count], refs[count : 2 * count]
    line_send, other_send, last_send, line_recv, pair_recv = refs[2 * count :]
    me = lax.axis_index("dp")
    place, one, two = place_of(me)
    for piece in range(count):
        full[piece][me] = mine[piece][...]
    greet(me, place, one, two)

    def remote(piece, block, send_sem, recv_sem, partner):
        return pltpu.make_async_remote_copy(
            src_ref=full[piece].at[block],
            dst_ref=full[piece].at[block],
            send_sem=send_sem,
            recv_sem=recv_sem,
            device_id={"dp": partner},
            device_id_type=MESH,
        )

    def pair(piece):
        if LAST_TWO[piece]:
            return two, one, me + 1 - 2 * two, me + 2 - 4 * one
        return one, two, me + 2 - 4 * one, me + 1 - 2 * two

    def up_copy(piece, at):
        block = at * 4 + one * 2 + two
        return remote(piece, block, line_send.at[piece, 0, at], line_recv.at[piece, at], me + 4)

    def down_copy(piece, at):
        block = at * 4 + one * 2 + two
        return remote(piece, block, line_send.at[piece, 1, at], line_recv.at[piece, at], me - 4)

    def other_copy(piece, at, incoming=False):
        last, other, _, partner = pair(piece)
        block = block_of(at, last, 1 - other if incoming else other, LAST_TWO[piece])
        return remote(piece, block, other_send.at[piece, at], pair_recv.at[piece, block], partner)

    def last_copy(piece, at, far, incoming=False):
        last, other, partner, _ = pair(piece)
        block = block_of(
            at, 1 - last if incoming else last, 1 - other if far else other, LAST_TWO[piece]
        )
        return remote(
            piece, block, last_send.at[piece, int(far), at], pair_recv.at[piece, block], partner
        )

    def at_level(level, act):
        if level == 0:
            act(place, 0)
            return

        @pl.when(place - level >= 0)
        def _():
            act(place - level, -1)

        @pl.when(place + level < LINE)
        def _():
            act(place + level, 1)

    def spread(at, side):
        for piece in range(count):
            if side < 0:
                up_copy(piece, at).wait_recv()
            if side > 0:
                down_copy(piece, at).wait_recv()
            if side <= 0:
                pl.when(place < LINE - 1)(lambda: up_copy(piece, at).start())
            if side >= 0:
                pl.when(place > 0)(lambda: down_copy(piece, at).start())
            other_copy(piece, at).start()
            last_copy(piece, at, False).start()

    def pass_on(at, side):
        for piece in range(count):
            other_copy(piece, at, True).wait_recv()
            last_copy(piece, at, True).start()

    def finish(at, side):
        for piece in range(count):
            last_copy(piece, at, False, True).wait_recv()
            last_copy(piece, at, True, True).wait_recv()
            if side <= 0:
                pl.when(place < LINE - 1)(lambda: up_copy(piece, at).wait_send())
            if side >= 0:
                pl.when(place > 0)(lambda: down_copy(piece, at).wait_send())
            other_copy(piece, at).wait_send()
            last_copy(piece, at, False).wait_send()
            last_copy(piece, at, True).wait_send()

    at_level(0, spread)
    for level in range(1, LINE):
        at_level(level, spread)
        at_level(level - 1, pass_on)
    at_level(LINE - 1, pass_on)
    for level in range(LINE):
        at_level(level, finish)


def gather_pieces(pieces):
    count = len(pieces)
    return pl.pallas_call(
        gather_kernel,
        out_shape=tuple(jax.ShapeDtypeStruct((SPAN, *p.shape), p.dtype) for p in pieces),
        in_specs=[pl.BlockSpec(memory_space=pltpu.VMEM)] * count,
        out_specs=tuple([pl.BlockSpec(memory_space=pltpu.VMEM)] * count),
        scratch_shapes=[
            pltpu.SemaphoreType.DMA((count, 2, LINE)),
            pltpu.SemaphoreType.DMA((count, LINE)),
            pltpu.SemaphoreType.DMA((count, 2, LINE)),
            pltpu.SemaphoreType.DMA((count, LINE)),
            pltpu.SemaphoreType.DMA((count, SPAN)),
        ],
        compiler_params=pltpu.CompilerParams(
            collective_id=0, has_side_effects=True, vmem_limit_bytes=VMEM_LIMIT
        ),
        name="gather",
    )(*pieces)


def scatter_kernel(*refs):
    count = len(LAST_TWO)
    parts, outs = refs[:count], refs[count : 2 * count]
    scratch = refs[2 * count :]
    first_in, second_out, second_in, up_out, down_out, up_in, down_in, total = (
        scratch[i * count : (i + 1) * count] for i in range(8)
    )
    first_send, first_recv, second_send, second_recv, line_send, line_recv = scratch[8 * count :]
    me = lax.axis_index("dp")
    place, one, two = place_of(me)
    greet(me, place, one, two)
    rows = parts[0].shape[1]

    def pair(piece):
        if LAST_TWO[piece]:
            return two, one, me + 1 - 2 * two, me + 2 - 4 * one
        return one, two, me + 2 - 4 * one, me + 1 - 2 * two

    def first_copy(piece, at, far):
        bit, other, partner, _ = pair(piece)
        block = block_of(at, 1 - bit, 1 - other if far else other, LAST_TWO[piece])
        return pltpu.make_async_remote_copy(
            src_ref=parts[piece].at[block],
            dst_ref=first_in[piece].at[int(far), at],
            send_sem=first_send.at[piece, int(far), at],
            recv_sem=first_recv.at[piece, int(far), at],
            device_id={"dp": partner},
            device_id_type=MESH,
        )

    def second_copy(piece, at):
        return pltpu.make_async_remote_copy(
            src_ref=second_out[piece].at[at],
            dst_ref=second_in[piece].at[at],
            send_sem=second_send.at[piece, at],
            recv_sem=second_recv.at[piece, at],
            device_id={"dp": pair(piece)[3]},
            device_id_type=MESH,
        )

    def line_copy(piece, at, side):
        return pltpu.make_async_remote_copy(
            src_ref=(up_out if side > 0 else down_out)[piece].at[at],
            dst_ref=(up_in if side > 0 else down_in)[piece].at[at],
            send_sem=line_send.at[piece, int(side > 0), at],
            recv_sem=line_recv.at[piece, int(side > 0), at],
            device_id={"dp": me + 4 * side},
            device_id_type=MESH,
        )

    def by_rows(act):
        @pl.loop(0, rows // 16)
        def _(step):
            act(pl.ds(pl.multiple_of(step * 16, 16), 16))

    def at_level(level, act):
        if level == 0:
            act(place, 0)
            return

        @pl.when(place - level >= 0)
        def _():
            act(place - level, -1)

        @pl.when(place + level < LINE)
        def _():
            act(place + level, 1)

    def begin(at, side):
        for piece in range(count):
            first_copy(piece, at, True).start()
            first_copy(piece, at, False).start()

    def second(at, side):
        for piece in range(count):
            bit, other, _, _ = pair(piece)
            block = block_of(at, bit, 1 - other, LAST_TWO[piece])
            first_copy(piece, at, True).wait_recv()

            def add(sl, piece=piece, block=block):
                second_out[piece][at, sl] = (
                    parts[piece][block, sl].astype(F32) + first_in[piece][1, at, sl].astype(F32)
                ).astype(BF16)

            by_rows(add)
            second_copy(piece, at).start()

    def third(at, side):
        for piece in range(count):
            first_copy(piece, at, False).wait_recv()
            second_copy(piece, at).wait_recv()

            def add(sl, piece=piece):
                total[piece][sl] = (
                    parts[piece][me + (at - place) * 4, sl].astype(F32)
                    + first_in[piece][0, at, sl].astype(F32)
                    + second_in[piece][at, sl].astype(F32)
                )

            by_rows(add)
            if side >= 0:

                @pl.when(place > 0)
                def _(piece=piece):
                    line_copy(piece, at, 1).wait_recv()

                    def add(sl):
                        total[piece][sl] += up_in[piece][at, sl].astype(F32)

                    by_rows(add)

            if side <= 0:

                @pl.when(place < LINE - 1)
                def _(piece=piece):
                    line_copy(piece, at, -1).wait_recv()

                    def add(sl):
                        total[piece][sl] += down_in[piece][at, sl].astype(F32)

                    by_rows(add)

            if side == 0:

                def put(sl, piece=piece):
                    outs[piece][sl] = total[piece][sl]

            else:

                def put(sl, piece=piece):
                    (up_out if side > 0 else down_out)[piece][at, sl] = total[piece][sl].astype(BF16)

            by_rows(put)
            if side != 0:
                line_copy(piece, at, side).start()

    def finish(at, side):
        for piece in range(count):
            first_copy(piece, at, True).wait_send()
            first_copy(piece, at, False).wait_send()
            second_copy(piece, at).wait_send()
            if side != 0:
                line_copy(piece, at, side).wait_send()

    for level in reversed(range(LINE)):
        at_level(level, begin)
    at_level(LINE - 1, second)
    for level in reversed(range(LINE)):
        if level > 0:
            at_level(level - 1, second)
        at_level(level, third)
    for level in range(LINE):
        at_level(level, finish)


def scatter_pieces(parts):
    count = len(parts)
    shapes = [p.shape[1:] for p in parts]

    def scratch(lead, dtype=BF16):
        return [pltpu.VMEM((*lead, *shape), dtype) for shape in shapes]

    line = (LINE,)
    return pl.pallas_call(
        scatter_kernel,
        out_shape=tuple(jax.ShapeDtypeStruct(shape, F32) for shape in shapes),
        in_specs=[pl.BlockSpec(memory_space=pltpu.VMEM)] * count,
        out_specs=tuple([pl.BlockSpec(memory_space=pltpu.VMEM)] * count),
        scratch_shapes=[
            *scratch((2, LINE)),
            *scratch(line),
            *scratch(line),
            *scratch(line),
            *scratch(line),
            *scratch(line),
            *scratch(line),
            *scratch((), F32),
            pltpu.SemaphoreType.DMA((count, 2, LINE)),
            pltpu.SemaphoreType.DMA((count, 2, LINE)),
            pltpu.SemaphoreType.DMA((count, LINE)),
            pltpu.SemaphoreType.DMA((count, LINE)),
            pltpu.SemaphoreType.DMA((count, 2, LINE)),
            pltpu.SemaphoreType.DMA((count, 2, LINE)),
        ],
        compiler_params=pltpu.CompilerParams(
            collective_id=1, has_side_effects=True, vmem_limit_bytes=VMEM_LIMIT
        ),
        name="scatter",
    )(*parts)


def gather_all(pieces):
    if lax.axis_size("dp") == SPAN:
        return tuple(full.reshape(-1, full.shape[-1]) for full in gather_pieces(pieces))
    return tuple(lax.all_gather(piece, "dp", axis=0, tiled=True) for piece in pieces)


def scatter_all(parts):
    if lax.axis_size("dp") == SPAN:
        return scatter_pieces(tuple(p.reshape(SPAN, -1, p.shape[-1]) for p in parts))
    return tuple(
        lax.psum_scatter(p.astype(F32), "dp", scatter_dimension=0, tiled=True) for p in parts
    )


def both_cores(partial_value):
    size = lax.axis_size("mp")
    total = partial_value
    moving = partial_value
    for _ in range(size - 1):
        moving = lax.ppermute(moving, "mp", [(i, (i + 1) % size) for i in range(size)])
        total = total + moving
    return total


def dot(a, b, a_axis=1, b_axis=0):
    return lax.dot_general(a, b, (((a_axis,), (b_axis,)), ((), ())), preferred_element_type=F32)


def body(
    hidden_in, lengths, cotangent, qkv_weight, qv_bias, out_weight, out_bias, attn_gain,
    attn_shift, up_weight, up_bias, down_weight, down_bias, ffn_gain, ffn_shift,
):
    seqs, span, feat = hidden_in.shape
    span_dp = lax.axis_size("dp")
    own = feat // span_dp
    width = qkv_weight.shape[3]
    units = up_weight.shape[2]
    heads = width // HEAD_DIM
    keymask = jnp.arange(span)[None, :] < lengths[:, None]
    rowmask = keymask.astype(F32).reshape(-1, 1)
    hidden = hidden_in.reshape(-1, feat)

    vectors = jnp.concatenate(
        [
            v.reshape(own, -1)
            for v in (
                out_bias, attn_gain, attn_shift, down_bias, ffn_gain, ffn_shift, qv_bias, up_bias
            )
        ],
        axis=1,
    )
    used = vectors.shape[1]
    vectors = jnp.pad(vectors, ((0, 0), (0, 128 - used)))
    qkv_w, up_w, down_t, out_t, small = gather_all(
        (
            qkv_weight.reshape(own, 3 * width),
            up_weight[0],
            down_weight[0].T,
            out_weight[0].T,
            vectors,
        )
    )
    small = small.T.astype(F32)
    out_b, gain_a, shift_a, down_b, gain_f, shift_f = (small[i : i + 1] for i in range(6))
    qv_b = small[6].reshape(span_dp, 2, -1).transpose(1, 0, 2).reshape(2, width)
    up_b = small[7:used].T.reshape(1, units)

    inputs_b = hidden.astype(BF16)
    projected = dot(inputs_b, qkv_w).reshape(seqs, span, 3, heads, HEAD_DIM)
    biases = qv_b.reshape(2, heads, HEAD_DIM)
    queries = (projected[:, :, 0] + biases[0]).astype(BF16)
    keys_b = projected[:, :, 1].astype(BF16)
    values = (projected[:, :, 2] + biases[1]).astype(BF16)
    scores = attend_scores(queries, keys_b, keymask)
    row_peak = jnp.max(scores, axis=-1, keepdims=True)
    logsum = row_peak + jnp.log(jnp.sum(jnp.exp(scores - row_peak), axis=-1, keepdims=True))
    probs_f = jnp.exp(scores - logsum)
    probs_b = probs_f.astype(BF16)
    context = jnp.einsum("bhqk,bkhe->bqhe", probs_b, values, preferred_element_type=F32)
    context = context.astype(BF16).reshape(seqs * span, width)
    attended = both_cores(dot(context, out_t, 1, 1)) + out_b
    mid, scaled_a, inverse_a = normalize(hidden + attended, gain_a, shift_a)
    mid_b = mid.astype(BF16)
    pre_act = dot(mid_b, up_w) + up_b
    act_b = gelu_exact(pre_act).astype(BF16)
    mlp_out = both_cores(dot(act_b, down_t, 1, 1)) + down_b
    output, scaled_f, inverse_f = normalize(mid + mlp_out, gain_f, shift_f)
    hidden_out = (output * rowmask).reshape(seqs, span, feat)

    upstream = cotangent.reshape(-1, feat) * rowmask
    d_resid_f, grad_gain_f, grad_shift_f = normalize_back(upstream, scaled_f, inverse_f, gain_f)
    grad_down_b = jnp.sum(d_resid_f, axis=0)
    mlp_b = d_resid_f.astype(BF16)
    grad_down = dot(mlp_b, act_b, 0, 0)
    d_pre = dot(mlp_b, down_t) * gelu_slope(pre_act)
    d_pre_b = d_pre.astype(BF16)
    grad_up = dot(mid_b, d_pre_b, 0, 0)
    grad_up_b = jnp.sum(d_pre, axis=0)
    d_mid = d_resid_f + both_cores(dot(d_pre_b, up_w, 1, 1))
    d_resid_a, grad_gain_a, grad_shift_a = normalize_back(d_mid, scaled_a, inverse_a, gain_a)
    grad_out_b = jnp.sum(d_resid_a, axis=0)
    attn_b = d_resid_a.astype(BF16)
    grad_out = dot(attn_b, context, 0, 0)
    d_context = dot(attn_b, out_t).astype(BF16).reshape(seqs, span, heads, HEAD_DIM)
    d_probs = jnp.einsum("bqhe,bkhe->bhqk", d_context, values, preferred_element_type=F32)
    d_values = jnp.einsum("bhqk,bqhe->bkhe", probs_b, d_context, preferred_element_type=F32)
    centred = jnp.sum(probs_f * d_probs, axis=-1, keepdims=True)
    d_scores = (probs_f * (d_probs - centred) * 0.125).astype(BF16)
    d_queries = jnp.einsum("bhqk,bkhe->bqhe", d_scores, keys_b, preferred_element_type=F32)
    d_keys = jnp.einsum("bhqk,bqhe->bkhe", d_scores, queries, preferred_element_type=F32)
    grad_qv = jnp.stack(
        [jnp.sum(d_queries, axis=(0, 1)).reshape(-1), jnp.sum(d_values, axis=(0, 1)).reshape(-1)]
    )
    d_proj = (
        jnp.stack([d_queries, d_keys, d_values], axis=2)
        .astype(BF16)
        .reshape(seqs * span, 3 * width)
    )
    grad_qkv = dot(inputs_b, d_proj, 0, 0)
    grad_input = (d_resid_a + both_cores(dot(d_proj, qkv_w, 1, 1))).reshape(seqs, span, feat)

    grad_small = jnp.concatenate(
        [
            v.reshape(feat, -1)
            for v in (
                grad_out_b, grad_gain_a, grad_shift_a, grad_down_b, grad_gain_f, grad_shift_f,
                grad_qv.reshape(2, span_dp, -1).transpose(1, 0, 2), grad_up_b,
            )
        ],
        axis=1,
    )
    grad_small = jnp.pad(grad_small, ((0, 0), (0, 128 - used)))
    qkv_g, up_g, down_g, out_g, small_g = scatter_all(
        tuple(g.astype(BF16) for g in (grad_qkv, grad_up, grad_down, grad_out, grad_small))
    )
    vec = [small_g[:, i].reshape(1, own) for i in range(6)]
    return (
        hidden_out,
        grad_input,
        qkv_g.reshape(1, own, 3, width),
        small_g[:, 6].reshape(1, 2, -1),
        out_g.T[None],
        vec[0],
        vec[1],
        vec[2],
        up_g[None],
        small_g[:, 7:used].reshape(1, -1),
        down_g.T[None],
        vec[3],
        vec[4],
        vec[5],
    )


def solution(mesh):
    return jax.shard_map(
        body,
        mesh=mesh,
        in_specs=(
            P("dp", None, None),
            P("dp"),
            P("dp", None, None),
            P(None, "dp", None, "mp"),
            P(None, None, ("mp", "dp")),
            P(None, "mp", "dp"),
            P(None, "dp"),
            P(None, "dp"),
            P(None, "dp"),
            P(None, "dp", "mp"),
            P(None, ("mp", "dp")),
            P(None, "mp", "dp"),
            P(None, "dp"),
            P(None, "dp"),
            P(None, "dp"),
        ),
        out_specs=(
            P("dp", None, None),
            P("dp", None, None),
            P(None, "dp", None, "mp"),
            P(None, None, ("mp", "dp")),
            P(None, "mp", "dp"),
            P(None, "dp"),
            P(None, "dp"),
            P(None, "dp"),
            P(None, "dp", "mp"),
            P(None, ("mp", "dp")),
            P(None, "mp", "dp"),
            P(None, "dp"),
            P(None, "dp"),
            P(None, "dp"),
        ),
        check_vma=False,
    )
```

time: 854 us -> 222 us (0.26)
  waiting for transfers between devices: 526 us -> 1.35 us
  blocking collectives: 249 us -> 0 us
  Pallas kernels: 0 us -> 152 us
  between operations: 18.4 us -> 1.81 us
    reduce_scatter x8 -> x0, waiting for transfers between devices: 472 us -> none  [the longest x1 143 us: scatter_layer(): lax.psum_scatter(grads[6], 'dp', scatter_dimension=0, tiled=True)]
    pallas_call x0 -> x2, Pallas kernels: none -> 152 us  [the longest x1 80.2 us: scatter_pieces(): pl.pallas_call(scatter_kernel, out_shape=tuple((jax.ShapeDtypeStruct(shap...]
    unnamed x2 -> x0, blocking collectives: 151 us -> none
    all_gather x7 -> x0, blocking collectives: 94.9 us -> none  [the longest x1 43.7 us: fetch_layer(): lax.all_gather(picked[1], 'dp', axis=1, tiled=True)]
    all_gather x3 -> x0, waiting for transfers between devices: 52 us -> none  [the longest x1 52 us: fetch_layer(): lax.all_gather(picked[8], 'dp', axis=1, tiled=True)]
    reshape x1 -> x19, local copies, waits for them, and re-layouts: 2.97 us -> 12.1 us  [the longest x8 5.42 us: body(): v.reshape(own, -1)]
  transfers between devices with their start and end apart: 11 -> 4, of which waited for: 7 -> 1; matrix products, arithmetic and copies ran while one was open for 3% -> 11% of each run, Pallas kernels for 0% -> 36%
where the time goes in v1:
time: 222 us; the launch traced here: 221 us
  Pallas kernels  152 us (68%)
  local copies, waits for them, and re-layouts  28.1 us (13%)
  matrix products  26.3 us (12%)
  other arithmetic  9.97 us (4%)
    pallas_call x1, Pallas kernels, scatter_pieces(): pl.pallas_call(scatter_kernel, out_shape=tuple((jax.ShapeDtypeStruct(shap...  80.2 us
    pallas_call x1, Pallas kernels, gather_pieces(): pl.pallas_call(gather_kernel, out_shape=tuple((jax.ShapeDtypeStruct((SPAN...  71.9 us
    dot_general x12, matrix products, dot(): lax.dot_general(a, b, (((a_axis,), (b_axis,)), ((), ())), preferred_eleme...  19 us
    unnamed x74, local copies, waits for them, and re-layouts  5.73 us
    reshape x8, local copies, waits for them, and re-layouts, body(): v.reshape(own, -1)  5.42 us
    reshape x9, local copies, waits for them, and re-layouts, body(): v.reshape(feat, -1)  4.96 us
  transfers between devices with their start and end apart: 4, of which 1 were waited for; matrix products, arithmetic and copies ran while one was open for 11% of the time, Pallas kernels for 36%

profile of v1, /device:TPU:0, one launch (start us, length us, event | category | flops | bytes accessed | tf_op | source)
XLA Modules:
  0.0 220.8 jit_solution(8053800862854089193)
XLA Ops:
  0.7 1.0 copy.82
  2.3 0.8 copy.83
  3.1 0.8 copy.84
  3.8 0.8 copy.85
  4.6 0.8 copy.86
  5.3 0.8 copy.87
  6.1 0.8 copy.88
  6.9 0.8 reshape.408
  8.1 1.3 reduce.45
  10.3 71.9 %gather.1 = (bf16[16,48,1152]{2,1,0:T(8,128)(2,1)}, bf16[16,48,1536]{2,1,0:T(8,128)(2,1)}, bf16[16,48,1536]{2,1,0:T(8,128)(2,1)}, bf16[16,48,384]{2,1,0:T(8,128)(2,1)}, bf16[16,48,128]{2,1,0:T(8,128)(2,1)}) custom-call(bf16[48,1152]{1,0:T(8,128)(2,1)} %bitcast.180, bf16[48,1536]{1,0:T(8,128)(2,1)} %bitcast.183, bf16[48,1536]{1,0:T(8,128)(2,1)} %bitcast.184, ...), custom_call_target="tpu_custom_call" | custom-call | tf_op jit(solution)/shard_map/gather/pallas_call | solution.py:193
  82.3 1.0 bitcast_convert_fusion
  83.4 0.7 slice_reduce_fusion.10
  85.0 2.1 fusion.25
  88.2 1.3 convolution_convert_fusion.6
  89.5 2.2 fusion.71
  91.7 1.4 slice_bitcast_fusion.2
  93.1 0.9 copy.92
  94.0 0.8 add.153
  94.8 1.3 fusion.62
  96.3 1.4 multiply_convert_fusion
  97.8 0.9 fusion.72
  99.2 1.3 collective-permute-done.1
  101.4 1.0 fusion.59
  102.3 1.3 fusion.66
  103.6 1.6 fusion.28
  105.7 2.2 %convolution_convert_fusion = bf16[768,1536]{1,0:T(8,128)(2,1)} fusion(bf16[128,1536]{1,0:T(8,128)(2,1)S(1)} %get-tuple-element.130, f32[128,768]{1,0:T(8,128)S(1)} %get-tuple-element.115), kind=kOutput, calls=%fused_computation.1 | convolution fusion | flops 303267840 | bytes 3145728 | tf_op jit(solution)/shard_map/dot_general | solution.py:428
  110.0 0.7 copy.98
  110.8 3.3 %convolution_convert_fusion.1 = bf16[768,1536]{1,0:T(8,128)(2,1)} fusion(bf16[128,1536]{1,0:T(8,128)(2,1)} %copy-done.9, f32[128,768]{1,0:T(8,128)S(1)} %get-tuple-element.122, f32[768]{0:T(1024)S(1)} %get-tuple-element.101, f32[768]{0:T(1024)S(1)} %get-tuple-element.102, f32[128]{0:T(128)S(1)} %copy-done.25, f32[128]{0:T(128)S(1)} %copy-done.18), kind=kOutput, calls=%fused_computation.2 | convolution fusion | flops 303661056 | bytes 3152896 | tf_op jit(solution)/shard_map/dot_general | solution.py:428
  114.1 1.9 multiply_reduce_fusion.2
  116.0 0.8 fusion.60
  117.4 1.2 fusion.47
  118.6 1.2 convolution_convert_fusion.3
  119.8 1.4 fusion.6
  121.2 2.8 %fusion.63 = (bf16[6,64]{1,0:T(8,128)(2,1)}, bf16[1,128,1,6,64]{1,4,3,2,0:T(8,128)(2,1)S(1)}, bf16[1,128,1,6,64]{1,4,3,2,0:T(8,128)(2,1)}, bf16[6,64]{1,0:T(8,128)(2,1)}) fusion(f32[1,128,6,64]{1,3,2,0:T(8,128)S(1)} %convolution_bitcast_fusion, f32[6,128,128]{1,2,0:T(8,128)} %fusion.47, f32[6,128,128]{1,2,0:T(8,128)S(1)} %get-tuple-element.129, ...), kind=kOutput, calls=%fused_computation.120 | convolution fusion | flops 13467775 | bytes 2074112 | tf_op jit(solution)/shard_map/bhqk,bkhe->bqhe/dot_general | solution.py:511
  124.0 0.9 pad_maximum_fusion
  125.8 0.7 reshape.396
  127.1 0.7 reshape.398
  128.2 0.9 concatenate.19
  129.2 0.7 pad.10.clone
  129.9 1.9 convolution_convert_fusion.2
  131.8 80.2 %scatter.1 = (f32[48,1152]{1,0:T(8,128)}, f32[48,1536]{1,0:T(8,128)}, f32[48,1536]{1,0:T(8,128)}, f32[48,384]{1,0:T(8,128)}, f32[48,128]{1,0:T(8,128)}) custom-call(bf16[16,48,1152]{2,1,0:T(8,128)(2,1)} %bitcast.157, bf16[16,48,1536]{2,1,0:T(8,128)(2,1)} %bitcast.154, bf16[16,48,1536]{2,1,0:T(8,128)(2,1)} %bitcast.153, bf16[16,48,384]{2,1,0:T(8,128)(2,1)} %bitcast.167, ...), custom_call_target="tpu_custom_call" | custom-call | tf_op jit(solution)/shard_map/scatter/pallas_call | solution.py:375
  212.0 1.1 reshape.405
  213.1 0.7 copy.100
  213.8 0.8 slice.83
  214.6 2.0 slice_reduce_fusion
  217.9 0.8 add_bitcast_fusion
  219.3 0.7 copy.112
  220.0 0.7 copy.113
  (118 shorter events, 12.1 us)
Async XLA Ops:
  0.6 84.4 %copy-start.2 = (f32[1,128,768]{2,1,0:T(8,128)S(1)}, f32[1,128,768]{2,1,0:T(8,128)}, u32[]{:S(2)}) copy-start(f32[1,128,768]{2,1,0:T(8,128)} %param.15) | copy-start | bytes 1179652
  83.4 4.2 %copy-start.12 = (f32[768,128]{0,1:T(8,128)}, f32[768,128]{0,1:T(8,128)S(1)}, u32[]{:S(2)}) copy-start(f32[768,128]{0,1:T(8,128)S(1)} %copy.90) | copy-start | bytes 1179652
  84.3 7.3 %copy-start.20 = (f32[6,64]{1,0:T(8,128)}, f32[6,64]{1,0:T(8,128)S(1)}, u32[]{:S(2)}) copy-start(f32[6,64]{1,0:T(8,128)S(1)} %add.140) | copy-start | bytes 4612
  87.2 0.8 copy-start.4
  88.1 8.2 %copy-start = (bf16[16,48,1536]{2,1,0:T(8,128)(2,1)S(1)}, bf16[16,48,1536]{2,1,0:T(8,128)(2,1)}, u32[]{:S(2)}) copy-start(bf16[16,48,1536]{2,1,0:T(8,128)(2,1)} %get-tuple-element.27) | copy-start | bytes 7077892
  89.5 2.2 %copy-start.10 = (bf16[6,64,128]{2,1,0:T(8,128)(2,1)}, bf16[6,64,128]{2,1,0:T(8,128)(2,1)S(1)}, u32[]{:S(2)}) copy-start(bf16[6,64,128]{2,1,0:T(8,128)(2,1)S(1)} %convolution_convert_fusion.6) | copy-start | bytes 294916
  91.7 3.1 %collective-permute-start = (f32[128,768]{1,0:T(8,128)}, f32[128,768]{1,0:T(8,128)}, u32[]{:S(2)}, u32[]{:S(2)}) collective-permute-start(f32[128,768]{1,0:T(8,128)} %fusion.71), channel_id=1, source_target_pairs={{0,1},{1,0},{2,3},{3,2},{4,5},{5,4},{6,7},{7,6},{8,9},{9,8},{10,11... | collective-permute-start | bytes 1179656 | tf_op jit(solution)/shard_map/ppermute | solution.py:422
  96.1 1.7 copy-start.6
  96.1 4.5 %copy-start.17 = (f32[128]{0:T(128)}, f32[128]{0:T(128)S(1)}, u32[]{:S(2)}) copy-start(f32[128]{0:T(128)S(1)} %broadcast_multiply_fusion.5) | copy-start | bytes 1540
  96.3 4.3 %copy-start.24 = (f32[128]{0:T(128)}, f32[128]{0:T(128)S(1)}, u32[]{:S(2)}) copy-start(f32[128]{0:T(128)S(1)} %add_rsqrt_fusion.1) | copy-start | bytes 1540
  97.7 2.9 %copy-start.23 = (f32[768]{0:T(1024)S(1)}, f32[768]{0:T(1024)}, u32[]{:S(2)}) copy-start(f32[768]{0:T(1024)} %get-tuple-element.100) | copy-start | bytes 9220
  97.7 3.3 %copy-start.8 = (f32[1,128,768]{2,1,0:T(8,128)S(1)}, f32[1,128,768]{2,1,0:T(8,128)}, u32[]{:S(2)}) copy-start(f32[1,128,768]{2,1,0:T(8,128)} %param.17) | copy-start | bytes 1179652
  97.7 3.3 %copy-start.16 = (f32[768]{0:T(1024)S(1)}, f32[768]{0:T(1024)}, u32[]{:S(2)}) copy-start(f32[768]{0:T(1024)} %get-tuple-element.98) | copy-start | bytes 9220
  97.7 3.6 %copy-start.22 = (f32[768]{0:T(1024)S(1)}, f32[768]{0:T(1024)}, u32[]{:S(2)}) copy-start(f32[768]{0:T(1024)} %get-tuple-element.99) | copy-start | bytes 9220
  98.6 1.9 collective-permute-start.1
  103.6 4.2 %copy-start.9 = (bf16[128,1536]{1,0:T(8,128)(2,1)}, bf16[128,1536]{1,0:T(8,128)(2,1)S(1)}, u32[]{:S(2)}) copy-start(bf16[128,1536]{1,0:T(8,128)(2,1)S(1)} %get-tuple-element.133) | copy-start | bytes 1179652
  105.3 4.4 %copy-start.30 = (bf16[1536]{0:T(1024)(128)(2,1)S(1)}, bf16[1536]{0:T(1024)(128)(2,1)}, u32[]{:S(2)}) copy-start(bf16[1536]{0:T(1024)(128)(2,1)} %get-tuple-element.132) | copy-start | bytes 9220
  105.3 5.5 %copy-start.18 = (f32[128]{0:T(128)S(1)}, f32[128]{0:T(128)}, u32[]{:S(2)}) copy-start(f32[128]{0:T(128)} %copy-done.17) | copy-start | bytes 1540
  105.3 5.5 %copy-start.25 = (f32[128]{0:T(128)S(1)}, f32[128]{0:T(128)}, u32[]{:S(2)}) copy-start(f32[128]{0:T(128)} %copy-done.24) | copy-start | bytes 1540
  105.3 8.8 %collective-permute-start.2 = (f32[128,768]{1,0:T(8,128)}, f32[128,768]{1,0:T(8,128)S(1)}, u32[]{:S(2)}, u32[]{:S(2)}) collective-permute-start(f32[128,768]{1,0:T(8,128)} %fusion.28), channel_id=1, source_target_pairs={{0,1},{1,0},{2,3},{3,2},{4,5},{5,4},{6,7},{7,6},{8,9},{9,8},{10,11... | collective-permute-start | bytes 1179656 | tf_op jit(solution)/shard_map/ppermute | solution.py:422
  110.7 5.2 %copy-start.19 = (f32[128]{0:T(128)S(1)}, f32[128]{0:T(128)}, u32[]{:S(2)}) copy-start(f32[128]{0:T(128)} %copy-done.17) | copy-start | bytes 1540
  110.7 5.2 %copy-start.26 = (f32[128]{0:T(128)S(1)}, f32[128]{0:T(128)}, u32[]{:S(2)}) copy-start(f32[128]{0:T(128)} %copy-done.24) | copy-start | bytes 1540
  114.1 2.7 %copy-start.7 = (bf16[16,48,384]{2,1,0:T(8,128)(2,1)S(1)}, bf16[16,48,384]{2,1,0:T(8,128)(2,1)}, u32[]{:S(2)}) copy-start(bf16[16,48,384]{2,1,0:T(8,128)(2,1)} %get-tuple-element.26) | copy-start | bytes 1769476
  114.1 3.4 %copy-start.5 = (f32[1152,128]{1,0:T(8,128)S(1)}, f32[1152,128]{1,0:T(8,128)}, u32[]{:S(2)}) copy-start(f32[1152,128]{1,0:T(8,128)} %copy-done.4) | copy-start | bytes 1769476
  116.0 2.6 %copy-start.11 = (bf16[6,64,128]{2,1,0:T(8,128)(2,1)S(1)}, bf16[6,64,128]{2,1,0:T(8,128)(2,1)}, u32[]{:S(2)}) copy-start(bf16[6,64,128]{2,1,0:T(8,128)(2,1)} %copy-done.10) | copy-start | bytes 294916
  116.0 3.8 %copy-start.21 = (f32[6,64]{1,0:T(8,128)S(1)}, f32[6,64]{1,0:T(8,128)}, u32[]{:S(2)}) copy-start(f32[6,64]{1,0:T(8,128)} %copy-done.20) | copy-start | bytes 4612
  117.2 7.8 %copy-start.1 = (bf16[16,48,1152]{2,1,0:T(8,128)(2,1)S(1)}, bf16[16,48,1152]{2,1,0:T(8,128)(2,1)}, u32[]{:S(2)}) copy-start(bf16[16,48,1152]{2,1,0:T(8,128)(2,1)} %get-tuple-element.24) | copy-start | bytes 5308420
  119.8 8.3 %copy-start.27 = (bf16[768,1]{0,1:T(2,128)(2,1)S(1)}, bf16[768,1]{0,1:T(2,128)(2,1)}, u32[]{:S(2)}) copy-start(bf16[768,1]{0,1:T(2,128)(2,1)} %reshape.399) | copy-start | bytes 4612
  119.8 8.3 %copy-start.28 = (bf16[768,1]{0,1:T(2,128)(2,1)S(1)}, bf16[768,1]{0,1:T(2,128)(2,1)}, u32[]{:S(2)}) copy-start(bf16[768,1]{0,1:T(2,128)(2,1)} %reshape.400) | copy-start | bytes 4612
  121.2 6.9 %copy-start.29 = (bf16[768,1]{0,1:T(2,128)(2,1)S(1)}, bf16[768,1]{0,1:T(2,128)(2,1)}, u32[]{:S(2)}) copy-start(bf16[768,1]{0,1:T(2,128)(2,1)} %reshape.401) | copy-start | bytes 4612
  121.2 8.7 %copy-start.3 = (f32[1,128,768]{2,1,0:T(8,128)S(1)}, f32[1,128,768]{2,1,0:T(8,128)}, u32[]{:S(2)}) copy-start(f32[1,128,768]{2,1,0:T(8,128)} %param.15) | copy-start | bytes 1179652
  124.0 3.8 %copy-start.32 = (bf16[6,64]{1,0:T(8,128)(2,1)S(1)}, bf16[6,64]{1,0:T(8,128)(2,1)}, u32[]{:S(2)}) copy-start(bf16[6,64]{1,0:T(8,128)(2,1)} %get-tuple-element.135) | copy-start | bytes 2308
  124.0 3.9 %copy-start.31 = (bf16[6,64]{1,0:T(8,128)(2,1)S(1)}, bf16[6,64]{1,0:T(8,128)(2,1)}, u32[]{:S(2)}) copy-start(bf16[6,64]{1,0:T(8,128)(2,1)} %get-tuple-element.124) | copy-start | bytes 2308
  125.6 92.3 %collective-permute-start.3 = (f32[128,768]{1,0:T(8,128)S(1)}, f32[128,768]{1,0:T(8,128)S(1)}, u32[]{:S(2)}, u32[]{:S(2)}) collective-permute-start(f32[128,768]{1,0:T(8,128)S(1)} %fusion.73), channel_id=1, source_target_pairs={{0,1},{1,0},{2,3},{3,2},{4,5},{5,4},{6,7},{7,6},{8,9},{9,8},{10,11... | collective-permute-start | bytes 1179656 | tf_op jit(solution)/shard_map/ppermute | solution.py:422
  212.0 6.7 %copy-start.15 = (f32[48,384]{1,0:T(8,128)S(1)}, f32[48,384]{1,0:T(8,128)}, u32[]{:S(2)}) copy-start(f32[48,384]{1,0:T(8,128)} %get-tuple-element.31) | copy-start | bytes 221188
  212.0 7.3 %copy-start.14 = (f32[48,1536]{1,0:T(8,128)S(1)}, f32[48,1536]{1,0:T(8,128)}, u32[]{:S(2)}) copy-start(f32[48,1536]{1,0:T(8,128)} %get-tuple-element.32) | copy-start | bytes 884740
  212.0 8.0 %copy-start.13 = (f32[48,1536]{1,0:T(8,128)S(1)}, f32[48,1536]{1,0:T(8,128)}, u32[]{:S(2)}) copy-start(f32[48,1536]{1,0:T(8,128)} %get-tuple-element.33) | copy-start | bytes 884740

commit v2 on v1

--- a/solution.py
+++ b/solution.py
@@ -160,6 +160,7 @@
             if side >= 0:
                 pl.when(place > 0)(lambda: down_copy(piece, at).start())
             other_copy(piece, at).start()
+        for piece in range(count):
             last_copy(piece, at, False).start()
 
     def pass_on(at, side):
@@ -220,7 +221,6 @@
     me = lax.axis_index("dp")
     place, one, two = place_of(me)
     greet(me, place, one, two)
-    rows = parts[0].shape[1]
 
     def pair(piece):
         if LAST_TWO[piece]:
@@ -259,8 +259,8 @@
             device_id_type=MESH,
         )
 
-    def by_rows(act):
-        @pl.loop(0, rows // 16)
+    def by_rows(piece, act):
+        @pl.loop(0, parts[piece].shape[1] // 16)
         def _(step):
             act(pl.ds(pl.multiple_of(step * 16, 16), 16))
 
@@ -280,6 +280,7 @@
     def begin(at, side):
         for piece in range(count):
             first_copy(piece, at, True).start()
+        for piece in range(count):
             first_copy(piece, at, False).start()
 
     def second(at, side):
@@ -293,7 +294,7 @@
                     parts[piece][block, sl].astype(F32) + first_in[piece][1, at, sl].astype(F32)
                 ).astype(BF16)
 
-            by_rows(add)
+            by_rows(piece, add)
             second_copy(piece, at).start()
 
     def third(at, side):
@@ -308,7 +309,7 @@
                     + second_in[piece][at, sl].astype(F32)
                 )
 
-            by_rows(add)
+            by_rows(piece, add)
             if side >= 0:
 
                 @pl.when(place > 0)
@@ -318,7 +319,7 @@
                     def add(sl):
                         total[piece][sl] += up_in[piece][at, sl].astype(F32)
 
-                    by_rows(add)
+                    by_rows(piece, add)
 
             if side <= 0:
 
@@ -329,7 +330,7 @@
                     def add(sl):
                         total[piece][sl] += down_in[piece][at, sl].astype(F32)
 
-                    by_rows(add)
+                    by_rows(piece, add)
 
             if side == 0:
 
@@ -341,7 +342,7 @@
                 def put(sl, piece=piece):
                     (up_out if side > 0 else down_out)[piece][at, sl] = total[piece][sl].astype(BF16)
 
-            by_rows(put)
+            by_rows(piece, put)
             if side != 0:
                 line_copy(piece, at, side).start()
 
@@ -444,15 +445,15 @@
 
     vectors = jnp.concatenate(
         [
-            v.reshape(own, -1)
+            v.reshape(-1, own)
             for v in (
                 out_bias, attn_gain, attn_shift, down_bias, ffn_gain, ffn_shift, qv_bias, up_bias
             )
         ],
-        axis=1,
-    )
-    used = vectors.shape[1]
-    vectors = jnp.pad(vectors, ((0, 0), (0, 128 - used)))
+        axis=0,
+    )
+    used = vectors.shape[0]
+    vectors = jnp.pad(vectors, ((0, 16 - used), (0, 128 - own)))
     qkv_w, up_w, down_t, out_t, small = gather_all(
         (
             qkv_weight.reshape(own, 3 * width),
@@ -462,10 +463,11 @@
             vectors,
         )
     )
-    small = small.T.astype(F32)
-    out_b, gain_a, shift_a, down_b, gain_f, shift_f = (small[i : i + 1] for i in range(6))
-    qv_b = small[6].reshape(span_dp, 2, -1).transpose(1, 0, 2).reshape(2, width)
-    up_b = small[7:used].T.reshape(1, units)
+    small = small.reshape(span_dp, 16, 128)[:, :used, :own].astype(F32)
+    rows = small[:, :6].transpose(1, 0, 2).reshape(6, feat)
+    out_b, gain_a, shift_a, down_b, gain_f, shift_f = (rows[i : i + 1] for i in range(6))
+    qv_b = small[:, 6].reshape(span_dp, 2, -1).transpose(1, 0, 2).reshape(2, width)
+    up_b = small[:, 7:].reshape(1, units)
 
     inputs_b = hidden.astype(BF16)
     projected = dot(inputs_b, qkv_w).reshape(seqs, span, 3, heads, HEAD_DIM)
@@ -521,32 +523,33 @@
     grad_qkv = dot(inputs_b, d_proj, 0, 0)
     grad_input = (d_resid_a + both_cores(dot(d_proj, qkv_w, 1, 1))).reshape(seqs, span, feat)
 
+    grad_rows = jnp.stack(
+        [grad_out_b, grad_gain_a, grad_shift_a, grad_down_b, grad_gain_f, grad_shift_f]
+    )
     grad_small = jnp.concatenate(
         [
-            v.reshape(feat, -1)
-            for v in (
-                grad_out_b, grad_gain_a, grad_shift_a, grad_down_b, grad_gain_f, grad_shift_f,
-                grad_qv.reshape(2, span_dp, -1).transpose(1, 0, 2), grad_up_b,
-            )
+            grad_rows.reshape(6, span_dp, own).transpose(1, 0, 2),
+            grad_qv.reshape(2, span_dp, -1).transpose(1, 0, 2).reshape(span_dp, 1, own),
+            grad_up_b.reshape(span_dp, -1, own),
         ],
         axis=1,
     )
-    grad_small = jnp.pad(grad_small, ((0, 0), (0, 128 - used)))
+    grad_small = jnp.pad(grad_small, ((0, 0), (0, 16 - used), (0, 128 - own))).reshape(-1, 128)
     qkv_g, up_g, down_g, out_g, small_g = scatter_all(
         tuple(g.astype(BF16) for g in (grad_qkv, grad_up, grad_down, grad_out, grad_small))
     )
-    vec = [small_g[:, i].reshape(1, own) for i in range(6)]
+    vec = [small_g[i : i + 1, :own] for i in range(6)]
     return (
         hidden_out,
         grad_input,
         qkv_g.reshape(1, own, 3, width),
-        small_g[:, 6].reshape(1, 2, -1),
+        small_g[6, :own].reshape(1, 2, -1),
         out_g.T[None],
         vec[0],
         vec[1],
         vec[2],
         up_g[None],
-        small_g[:, 7:used].reshape(1, -1),
+        small_g[7:used, :own].reshape(1, -1),
         down_g.T[None],
         vec[3],
         vec[4],

time: 222 us -> 222 us (level)
  local copies, waits for them, and re-layouts: 28.1 us -> 23 us
  other arithmetic: 9.97 us -> 14.7 us
  matrix products: 26.3 us -> 29.9 us
    reshape x18 -> x5, local copies, waits for them, and re-layouts: 11 us -> 2.19 us  [the longest x2 0.82 us: body(): v.reshape(-1, own)]
    add x0 -> x4, local copies, waits for them, and re-layouts: none -> 3.47 us  [the longest x2 1.44 us: normalize(): return (scaled * gain_vec + shift_vec, scaled, inverse)]
    another operation x2 -> x9, local copies, waits for them, and re-layouts: 0.73 us -> 3.12 us  [the longest x7 2.39 us: body(): jnp.stack([grad_out_b, grad_gain_a, grad_shift_a, grad_down_b, grad_gain_...]
    transpose x3 -> x2, local copies, waits for them, and re-layouts: 2.27 us -> 0.01 us  [the longest x1 0.01 us: body(): grad_qv.reshape(2, span_dp, -1).transpose(1, 0, 2).reshape(span_dp, 1, own)]
    unnamed x74 -> x79, local copies, waits for them, and re-layouts: 5.73 us -> 6.14 us
  transfers between devices with their start and end apart: 4 -> 4, of which waited for: 1 -> 0; matrix products, arithmetic and copies ran while one was open for 11% -> 9% of each run, Pallas kernels for 36% -> 36%
where the time goes in v2:
time: 222 us; the launch traced here: 221 us
  Pallas kernels  150 us (68%)
  matrix products  29.9 us (13%)
  local copies, waits for them, and re-layouts  23 us (10%)
  other arithmetic  14.7 us (7%)
    pallas_call x1, Pallas kernels, scatter_pieces(): pl.pallas_call(scatter_kernel, out_shape=tuple((jax.ShapeDtypeStruct(shap...  78.8 us
    pallas_call x1, Pallas kernels, gather_pieces(): pl.pallas_call(gather_kernel, out_shape=tuple((jax.ShapeDtypeStruct((SPAN...  71.6 us
    dot_general x12, matrix products, dot(): lax.dot_general(a, b, (((a_axis,), (b_axis,)), ((), ())), preferred_eleme...  20.8 us
    unnamed x79, local copies, waits for them, and re-layouts  6.14 us
  transfers between devices with their start and end apart: 4, of which 0 were waited for; matrix products, arithmetic and copies ran while one was open for 9% of the time, Pallas kernels for 36%

profile of v2, /device:TPU:0, one launch (start us, length us, event | category | flops | bytes accessed | tf_op | source)
XLA Modules:
  0.0 220.9 jit_solution(11416132833829035591)
XLA Ops:
  0.6 1.0 copy.37
  2.8 1.3 reduce.49
  4.2 0.7 reshape.360
  4.9 0.8 concatenate.20
  6.4 71.6 %gather.1 = (bf16[16,48,1152]{2,1,0:T(8,128)(2,1)}, bf16[16,48,1536]{2,1,0:T(8,128)(2,1)}, bf16[16,48,1536]{2,1,0:T(8,128)(2,1)}, bf16[16,48,384]{2,1,0:T(8,128)(2,1)}, bf16[16,16,128]{2,1,0:T(8,128)(2,1)}) custom-call(bf16[48,1152]{1,0:T(8,128)(2,1)} %bitcast.161, bf16[48,1536]{1,0:T(8,128)(2,1)} %bitcast.164, bf16[48,1536]{1,0:T(8,128)(2,1)} %bitcast.165, ...), custom_call_target="tpu_custom_call" | custom-call | tf_op jit(solution)/shard_map/gather/pallas_call | solution.py:194
  78.0 0.9 slice_convert_fusion.1
  79.8 2.2 %fusion.25 = f32[1152,128]{1,0:T(8,128)S(1)} fusion(bf16[768,1152]{1,0:T(8,128)(2,1)} %bitcast.142, f32[1,128,768]{2,1,0:T(8,128)} %param.15), kind=kOutput, calls=%fused_computation.63 | convolution fusion | flops 226590720 | bytes 2752512 | tf_op jit(solution)/shard_map/dot_general | solution.py:429
  82.0 0.8 copy-done.6
  83.4 1.3 convolution_convert_fusion.6
  84.7 2.2 fusion.81
  86.9 0.7 slice_reduce_fusion.1
  87.6 0.7 add.145
  88.4 0.7 add.153
  89.1 1.3 fusion.71
  90.9 2.3 %multiply_convert_fusion = (bf16[128,1536]{1,0:T(8,128)(2,1)S(1)}, f32[128,1536]{1,0:T(8,128)}) fusion(f32[1536]{0:T(1024)} %add.153, bf16[768,1536]{1,0:T(8,128)(2,1)S(1)} %bitcast.139, f32[128,768]{1,0:T(8,128)S(1)} %get-tuple-element.86, f32[768]{0:T(1024)S(1)} %add.150, f32[768]{0:T(1024)S(1)} %mul.162, f32[128]{0:T(128)S(1)} %add_rsqrt_fusion.1, ...), kind=kOutput, calls=%fused_computation.24 | convolution fusion | flops 303661056 | bytes 3945472 | tf_op jit(solution)/shard_map/dot_general | solution.py:429
  93.2 1.6 fusion.82
  95.4 1.4 add.158
  96.7 1.4 mul.171
  98.1 1.4 add.163
  99.5 1.5 fusion.70
  101.2 1.9 multiply_reduce_fusion.1
  103.1 2.3 %fusion.68 = (bf16[768]{0:T(1024)(128)(2,1)}, f32[128,768]{1,0:T(8,128)S(1)}, f32[1,128,768]{2,1,0:T(8,128)}) fusion(f32[128]{0:T(128)S(1)} %broadcast_multiply_fusion.2, f32[128,768]{1,0:T(8,128)S(1)} %get-tuple-element.84, f32[128]{0:T(128)S(1)} %broadcast_multiply_fusion.4, f32[128]{0:T(128)S(1)} %broadcast_multiply_fusion.3, f32[768]{0:T(1024)} %mul.171, ...), kind=kLoop, calls=%fused_computation.121 | loop fusion | flops 1178880 | bytes 1583104 | tf_op jit(solution)/shard_map/reduce_sum | solution.py:496
  105.4 1.3 fusion.76
  106.7 1.6 fusion.28
  108.5 2.2 %convolution_convert_fusion = bf16[768,1536]{1,0:T(8,128)(2,1)} fusion(bf16[128,1536]{1,0:T(8,128)(2,1)S(1)} %get-tuple-element.101, f32[128,768]{1,0:T(8,128)S(1)} %get-tuple-element.79), kind=kOutput, calls=%fused_computation.1 | convolution fusion | flops 303267840 | bytes 3145728 | tf_op jit(solution)/shard_map/dot_general | solution.py:429
  110.7 0.7 stack.57
  111.4 0.7 stack.58
  112.1 0.7 stack.59
  112.8 0.7 reshape.377
  113.4 3.3 %convolution_convert_fusion.1 = bf16[768,1536]{1,0:T(8,128)(2,1)} fusion(bf16[128,1536]{1,0:T(8,128)(2,1)} %copy-done.12, f32[128,768]{1,0:T(8,128)S(1)} %get-tuple-element.86, f32[768]{0:T(1024)S(1)} %add.150, f32[768]{0:T(1024)S(1)} %mul.162, f32[128]{0:T(128)S(1)} %copy-done.28, f32[128]{0:T(128)S(1)} %copy-done.24), kind=kOutput, calls=%fused_computation.2 | convolution fusion | flops 303661056 | bytes 3152896 | tf_op jit(solution)/shard_map/dot_general | solution.py:429
  116.7 1.9 multiply_reduce_fusion.2
  118.6 0.7 fusion.69
  119.8 2.1 fusion.56
  121.9 0.9 convolution_bitcast_fusion
  122.8 1.2 convolution_convert_fusion.3
  124.1 2.2 fusion.6
  126.2 2.2 fusion.72
  128.4 1.0 pad_maximum_fusion
  129.5 1.9 convolution_convert_fusion.2
  133.3 0.7 fusion.51.refs_4_
  134.0 78.8 %scatter.1 = (f32[48,1152]{1,0:T(8,128)}, f32[48,1536]{1,0:T(8,128)}, f32[48,1536]{1,0:T(8,128)}, f32[48,384]{1,0:T(8,128)}, f32[16,128]{1,0:T(8,128)}) custom-call(bf16[16,48,1152]{2,1,0:T(8,128)(2,1)} %bitcast.141, bf16[16,48,1536]{2,1,0:T(8,128)(2,1)} %bitcast.138, bf16[16,48,1536]{2,1,0:T(8,128)(2,1)} %bitcast.137, bf16[16,48,384]{2,1,0:T(8,128)(2,1)} %bitcast.151, ...), custom_call_target="tpu_custom_call" | custom-call | tf_op jit(solution)/shard_map/scatter/pallas_call | solution.py:376
  212.8 1.1 reshape.378
  213.9 0.7 copy.51
  214.6 0.7 slice.97
  215.3 1.5 fusion.74
  218.0 0.8 add_bitcast_fusion
  219.4 0.7 copy.62
  220.1 0.7 copy.63
  (122 shorter events, 8.2 us)
Async XLA Ops:
  79.1 4.2 %copy-start.25 = (f32[6,64]{1,0:T(8,128)}, f32[6,64]{1,0:T(8,128)S(1)}, u32[]{:S(2)}) copy-start(f32[6,64]{1,0:T(8,128)S(1)} %add.140) | copy-start | bytes 4612
  79.8 9.4 %copy-start.4 = (f32[1,128,768]{2,1,0:T(8,128)S(1)}, f32[1,128,768]{2,1,0:T(8,128)}, u32[]{:S(2)}) copy-start(f32[1,128,768]{2,1,0:T(8,128)} %param.15) | copy-start | bytes 1179652
  82.0 0.8 copy-start.6
  83.2 7.7 %copy-start = (bf16[16,48,1536]{2,1,0:T(8,128)(2,1)S(1)}, bf16[16,48,1536]{2,1,0:T(8,128)(2,1)}, u32[]{:S(2)}) copy-start(bf16[16,48,1536]{2,1,0:T(8,128)(2,1)} %get-tuple-element.27) | copy-start | bytes 7077892
  84.7 4.4 %copy-start.13 = (bf16[6,64,128]{2,1,0:T(8,128)(2,1)}, bf16[6,64,128]{2,1,0:T(8,128)(2,1)S(1)}, u32[]{:S(2)}) copy-start(bf16[6,64,128]{2,1,0:T(8,128)(2,1)S(1)} %convolution_convert_fusion.6) | copy-start | bytes 294916
  86.9 2.2 %collective-permute-start = (f32[128,768]{1,0:T(8,128)}, f32[128,768]{1,0:T(8,128)}, u32[]{:S(2)}, u32[]{:S(2)}) collective-permute-start(f32[128,768]{1,0:T(8,128)} %fusion.81), channel_id=1, source_target_pairs={{0,1},{1,0},{2,3},{3,2},{4,5},{5,4},{6,7},{7,6},{8,9},{9,8},{10,11... | collective-permute-start | bytes 1179656 | tf_op jit(solution)/shard_map/ppermute | solution.py:423
  90.4 2.9 %copy-start.8 = (bf16[16,48,1536]{2,1,0:T(8,128)(2,1)S(1)}, bf16[16,48,1536]{2,1,0:T(8,128)(2,1)}, u32[]{:S(2)}) copy-start(bf16[16,48,1536]{2,1,0:T(8,128)(2,1)} %get-tuple-element.28) | copy-start | bytes 7077892
  90.4 0.5 copy-start.23
  90.6 2.6 %copy-start.27 = (f32[128]{0:T(128)}, f32[128]{0:T(128)S(1)}, u32[]{:S(2)}) copy-start(f32[128]{0:T(128)S(1)} %add_rsqrt_fusion.1) | copy-start | bytes 1540
  94.9 4.6 %collective-permute-start.1 = (f32[128,768]{1,0:T(8,128)}, f32[128,768]{1,0:T(8,128)}, u32[]{:S(2)}, u32[]{:S(2)}) collective-permute-start(f32[128,768]{1,0:T(8,128)} %fusion.82), channel_id=1, source_target_pairs={{0,1},{1,0},{2,3},{3,2},{4,5},{5,4},{6,7},{7,6},{8,9},{9,8},{10,11... | collective-permute-start | bytes 1179656 | tf_op jit(solution)/shard_map/ppermute | solution.py:423
  99.5 3.7 %copy-start.11 = (f32[1,128,768]{2,1,0:T(8,128)S(1)}, f32[1,128,768]{2,1,0:T(8,128)}, u32[]{:S(2)}) copy-start(f32[1,128,768]{2,1,0:T(8,128)} %param.17) | copy-start | bytes 1179652
  99.5 5.9 %copy-start.9 = (bf16[16,48,1536]{2,1,0:T(8,128)(2,1)S(1)}, bf16[16,48,1536]{2,1,0:T(8,128)(2,1)}, u32[]{:S(2)}) copy-start(bf16[16,48,1536]{2,1,0:T(8,128)(2,1)} %get-tuple-element.28) | copy-start | bytes 7077892
  99.5 5.9 %copy-start.15 = (f32[128,1536]{1,0:T(8,128)S(1)}, f32[128,1536]{1,0:T(8,128)}, u32[]{:S(2)}) copy-start(f32[128,1536]{1,0:T(8,128)} %get-tuple-element.102) | copy-start | bytes 2359300
  105.4 3.1 %copy-start.2 = (f32[128,768]{1,0:T(8,128)}, f32[128,768]{1,0:T(8,128)S(1)}, u32[]{:S(2)}) copy-start(f32[128,768]{1,0:T(8,128)S(1)} %get-tuple-element.79) | copy-start | bytes 1179652
  106.7 4.0 %copy-start.12 = (bf16[128,1536]{1,0:T(8,128)(2,1)}, bf16[128,1536]{1,0:T(8,128)(2,1)S(1)}, u32[]{:S(2)}) copy-start(bf16[128,1536]{1,0:T(8,128)(2,1)S(1)} %get-tuple-element.104) | copy-start | bytes 1179652
  108.3 2.4 %copy-start.34 = (bf16[768]{0:T(1024)(128)(2,1)S(1)}, bf16[768]{0:T(1024)(128)(2,1)}, u32[]{:S(2)}) copy-start(bf16[768]{0:T(1024)(128)(2,1)} %get-tuple-element.78) | copy-start | bytes 4612
  108.3 3.0 %copy-start.33 = (bf16[768]{0:T(1024)(128)(2,1)S(1)}, bf16[768]{0:T(1024)(128)(2,1)}, u32[]{:S(2)}) copy-start(bf16[768]{0:T(1024)(128)(2,1)} %get-tuple-element.62) | copy-start | bytes 4612
  108.3 3.7 %copy-start.32 = (bf16[768]{0:T(1024)(128)(2,1)S(1)}, bf16[768]{0:T(1024)(128)(2,1)}, u32[]{:S(2)}) copy-start(bf16[768]{0:T(1024)(128)(2,1)} %get-tuple-element.68) | copy-start | bytes 4612
  108.3 4.4 %copy-start.35 = (bf16[1536]{0:T(1024)(128)(2,1)S(1)}, bf16[1536]{0:T(1024)(128)(2,1)}, u32[]{:S(2)}) copy-start(bf16[1536]{0:T(1024)(128)(2,1)} %get-tuple-element.103) | copy-start | bytes 9220
  108.4 5.1 %copy-start.24 = (f32[128]{0:T(128)S(1)}, f32[128]{0:T(128)}, u32[]{:S(2)}) copy-start(f32[128]{0:T(128)} %copy-done.23) | copy-start | bytes 1540
  108.4 5.1 %copy-start.28 = (f32[128]{0:T(128)S(1)}, f32[128]{0:T(128)}, u32[]{:S(2)}) copy-start(f32[128]{0:T(128)} %copy-done.27) | copy-start | bytes 1540
  108.4 8.3 %collective-permute-start.2 = (f32[128,768]{1,0:T(8,128)}, f32[128,768]{1,0:T(8,128)S(1)}, u32[]{:S(2)}, u32[]{:S(2)}) collective-permute-start(f32[128,768]{1,0:T(8,128)} %fusion.28), channel_id=1, source_target_pairs={{0,1},{1,0},{2,3},{3,2},{4,5},{5,4},{6,7},{7,6},{8,9},{9,8},{10,11... | collective-permute-start | bytes 1179656 | tf_op jit(solution)/shard_map/ppermute | solution.py:423
  110.7 6.0 %copy-start.3 = (f32[128,768]{1,0:T(8,128)S(1)}, f32[128,768]{1,0:T(8,128)}, u32[]{:S(2)}) copy-start(f32[128,768]{1,0:T(8,128)} %copy-done.2) | copy-start | bytes 1179652
  116.7 2.6 %copy-start.10 = (bf16[16,48,384]{2,1,0:T(8,128)(2,1)S(1)}, bf16[16,48,384]{2,1,0:T(8,128)(2,1)}, u32[]{:S(2)}) copy-start(bf16[16,48,384]{2,1,0:T(8,128)(2,1)} %get-tuple-element.26) | copy-start | bytes 1769476
  118.6 4.2 %copy-start.14 = (bf16[6,64,128]{2,1,0:T(8,128)(2,1)S(1)}, bf16[6,64,128]{2,1,0:T(8,128)(2,1)}, u32[]{:S(2)}) copy-start(bf16[6,64,128]{2,1,0:T(8,128)(2,1)} %copy-done.13) | copy-start | bytes 294916
  118.6 5.4 %copy-start.26 = (f32[6,64]{1,0:T(8,128)S(1)}, f32[6,64]{1,0:T(8,128)}, u32[]{:S(2)}) copy-start(f32[6,64]{1,0:T(8,128)} %copy-done.25) | copy-start | bytes 4612
  119.3 4.7 %copy-start.7 = (f32[1152,128]{1,0:T(8,128)S(1)}, f32[1152,128]{1,0:T(8,128)}, u32[]{:S(2)}) copy-start(f32[1152,128]{1,0:T(8,128)} %copy-done.6) | copy-start | bytes 1769476
  119.7 9.7 %copy-start.5 = (f32[1,128,768]{2,1,0:T(8,128)S(1)}, f32[1,128,768]{2,1,0:T(8,128)}, u32[]{:S(2)}) copy-start(f32[1,128,768]{2,1,0:T(8,128)} %param.15) | copy-start | bytes 1179652
  124.1 7.4 %copy-start.1 = (bf16[16,48,1152]{2,1,0:T(8,128)(2,1)S(1)}, bf16[16,48,1152]{2,1,0:T(8,128)(2,1)}, u32[]{:S(2)}) copy-start(bf16[16,48,1152]{2,1,0:T(8,128)(2,1)} %get-tuple-element.24) | copy-start | bytes 5308420
  129.4 3.3 %copy-start.31 = (bf16[768]{0:T(1024)(128)(2,1)S(1)}, bf16[768]{0:T(1024)(128)(2,1)}, u32[]{:S(2)}) copy-start(bf16[768]{0:T(1024)(128)(2,1)} %get-tuple-element.80) | copy-start | bytes 4612
  129.5 3.4 %copy-start.30 = (bf16[768]{0:T(1024)(128)(2,1)S(1)}, bf16[768]{0:T(1024)(128)(2,1)}, u32[]{:S(2)}) copy-start(bf16[768]{0:T(1024)(128)(2,1)} %get-tuple-element.64) | copy-start | bytes 4612
  129.5 3.5 %copy-start.29 = (bf16[768]{0:T(1024)(128)(2,1)S(1)}, bf16[768]{0:T(1024)(128)(2,1)}, u32[]{:S(2)}) copy-start(bf16[768]{0:T(1024)(128)(2,1)} %get-tuple-element.69) | copy-start | bytes 4612
  129.5 3.7 %copy-start.20 = (bf16[1,16,48]{2,0,1:T(2,128)(2,1)S(1)}, bf16[1,16,48]{2,0,1:T(2,128)(2,1)}, u32[]{:S(2)}) copy-start(bf16[1,16,48]{2,0,1:T(2,128)(2,1)} %stack.57) | copy-start | bytes 4612
  129.5 3.7 %copy-start.21 = (bf16[1,16,48]{2,0,1:T(2,128)(2,1)S(1)}, bf16[1,16,48]{2,0,1:T(2,128)(2,1)}, u32[]{:S(2)}) copy-start(bf16[1,16,48]{2,0,1:T(2,128)(2,1)} %stack.58) | copy-start | bytes 4612
  129.5 3.7 %copy-start.22 = (bf16[1,16,48]{2,0,1:T(2,128)(2,1)S(1)}, bf16[1,16,48]{2,0,1:T(2,128)(2,1)}, u32[]{:S(2)}) copy-start(bf16[1,16,48]{2,0,1:T(2,128)(2,1)} %stack.59) | copy-start | bytes 4612
  129.5 3.8 %copy-start.19 = (bf16[16,2,48]{2,1,0:T(2,128)(2,1)S(1)}, bf16[16,2,48]{2,1,0:T(2,128)(2,1)}, u32[]{:S(2)}) copy-start(bf16[16,2,48]{2,1,0:T(2,128)(2,1)} %reshape.377) | copy-start | bytes 9220
  132.2 85.7 %collective-permute-start.3 = (f32[128,768]{1,0:T(8,128)S(1)}, f32[128,768]{1,0:T(8,128)S(1)}, u32[]{:S(2)}, u32[]{:S(2)}) collective-permute-start(f32[128,768]{1,0:T(8,128)S(1)} %fusion.83), channel_id=1, source_target_pairs={{0,1},{1,0},{2,3},{3,2},{4,5},{5,4},{6,7},{7,6},{8,9},{9,8},{10,11... | collective-permute-start | bytes 1179656 | tf_op jit(solution)/shard_map/ppermute | solution.py:423
  212.8 6.0 %copy-start.18 = (f32[48,384]{1,0:T(8,128)S(1)}, f32[48,384]{1,0:T(8,128)}, u32[]{:S(2)}) copy-start(f32[48,384]{1,0:T(8,128)} %get-tuple-element.31) | copy-start | bytes 221188
  212.8 6.7 %copy-start.17 = (f32[48,1536]{1,0:T(8,128)S(1)}, f32[48,1536]{1,0:T(8,128)}, u32[]{:S(2)}) copy-start(f32[48,1536]{1,0:T(8,128)} %get-tuple-element.32) | copy-start | bytes 884740
  212.8 7.4 %copy-start.16 = (f32[48,1536]{1,0:T(8,128)S(1)}, f32[48,1536]{1,0:T(8,128)}, u32[]{:S(2)}) copy-start(f32[48,1536]{1,0:T(8,128)} %get-tuple-element.33) | copy-start | bytes 884740

commit v3 on v2

--- a/solution.py
+++ b/solution.py
@@ -54,7 +54,7 @@
 LINE = 4
 SPAN = 16
 
-LAST_TWO = (True, True, False, False, False)
+LAST_TWO = (True, False, True, False, False, True)
 
 
 def place_of(me):
@@ -454,9 +454,10 @@
     )
     used = vectors.shape[0]
     vectors = jnp.pad(vectors, ((0, 16 - used), (0, 128 - own)))
-    qkv_w, up_w, down_t, out_t, small = gather_all(
+    qk_w, value_w, up_w, down_t, out_t, small = gather_all(
         (
-            qkv_weight.reshape(own, 3 * width),
+            qkv_weight[0, :, :2].reshape(own, 2 * width),
+            qkv_weight[0, :, 2],
             up_weight[0],
             down_weight[0].T,
             out_weight[0].T,
@@ -470,11 +471,12 @@
     up_b = small[:, 7:].reshape(1, units)
 
     inputs_b = hidden.astype(BF16)
-    projected = dot(inputs_b, qkv_w).reshape(seqs, span, 3, heads, HEAD_DIM)
+    projected = dot(inputs_b, qk_w).reshape(seqs, span, 2, heads, HEAD_DIM)
+    value_part = dot(inputs_b, value_w).reshape(seqs, span, heads, HEAD_DIM)
     biases = qv_b.reshape(2, heads, HEAD_DIM)
     queries = (projected[:, :, 0] + biases[0]).astype(BF16)
     keys_b = projected[:, :, 1].astype(BF16)
-    values = (projected[:, :, 2] + biases[1]).astype(BF16)
+    values = (value_part + biases[1]).astype(BF16)
     scores = attend_scores(queries, keys_b, keymask)
     row_peak = jnp.max(scores, axis=-1, keepdims=True)
     logsum = row_peak + jnp.log(jnp.sum(jnp.exp(scores - row_peak), axis=-1, keepdims=True))
@@ -515,13 +517,14 @@
     grad_qv = jnp.stack(
         [jnp.sum(d_queries, axis=(0, 1)).reshape(-1), jnp.sum(d_values, axis=(0, 1)).reshape(-1)]
     )
-    d_proj = (
-        jnp.stack([d_queries, d_keys, d_values], axis=2)
-        .astype(BF16)
-        .reshape(seqs * span, 3 * width)
-    )
-    grad_qkv = dot(inputs_b, d_proj, 0, 0)
-    grad_input = (d_resid_a + both_cores(dot(d_proj, qkv_w, 1, 1))).reshape(seqs, span, feat)
+    d_qk = (
+        jnp.stack([d_queries, d_keys], axis=2).astype(BF16).reshape(seqs * span, 2 * width)
+    )
+    d_value = d_values.astype(BF16).reshape(seqs * span, width)
+    grad_qk = dot(inputs_b, d_qk, 0, 0)
+    grad_value = dot(inputs_b, d_value, 0, 0)
+    input_part = dot(d_qk, qk_w, 1, 1) + dot(d_value, value_w, 1, 1)
+    grad_input = (d_resid_a + both_cores(input_part)).reshape(seqs, span, feat)
 
     grad_rows = jnp.stack(
         [grad_out_b, grad_gain_a, grad_shift_a, grad_down_b, grad_gain_f, grad_shift_f]
@@ -535,14 +538,14 @@
         axis=1,
     )
     grad_small = jnp.pad(grad_small, ((0, 0), (0, 16 - used), (0, 128 - own))).reshape(-1, 128)
-    qkv_g, up_g, down_g, out_g, small_g = scatter_all(
-        tuple(g.astype(BF16) for g in (grad_qkv, grad_up, grad_down, grad_out, grad_small))
+    qk_g, value_g, up_g, down_g, out_g, small_g = scatter_all(
+        tuple(g.astype(BF16) for g in (grad_qk, grad_value, grad_up, grad_down, grad_out, grad_small))
     )
     vec = [small_g[i : i + 1, :own] for i in range(6)]
     return (
         hidden_out,
         grad_input,
-        qkv_g.reshape(1, own, 3, width),
+        jnp.concatenate([qk_g, value_g], axis=1).reshape(1, own, 3, width),
         small_g[6, :own].reshape(1, 2, -1),
         out_g.T[None],
         vec[0],

time: 222 us -> 216 us (0.973)
  matrix products: 29.9 us -> 25.1 us
    pallas_call x1, Pallas kernels: 71.6 us -> 68.6 us  [gather_pieces(): pl.pallas_call(gather_kernel, out_shape=tuple((jax.ShapeDtypeStruct((SPAN...]
    dot_general x12 -> x15, matrix products: 20.8 us -> 19.7 us  [dot(): lax.dot_general(a, b, (((a_axis,), (b_axis,)), ((), ())), preferred_eleme...]
    unnamed x79 -> x66, local copies, waits for them, and re-layouts: 6.14 us -> 5.71 us
  transfers between devices with their start and end apart: 4 -> 4, of which waited for: 0 -> 1; matrix products, arithmetic and copies ran while one was open for 9% -> 7% of each run, Pallas kernels for 36% -> 37%
where the time goes in v3:
time: 216 us; the launch traced here: 215 us
  Pallas kernels  148 us (69%)
  matrix products  25.1 us (12%)
  local copies, waits for them, and re-layouts  23.2 us (11%)
  other arithmetic  14.8 us (7%)
    pallas_call x1, Pallas kernels, scatter_pieces(): pl.pallas_call(scatter_kernel, out_shape=tuple((jax.ShapeDtypeStruct(shap...  79.3 us
    pallas_call x1, Pallas kernels, gather_pieces(): pl.pallas_call(gather_kernel, out_shape=tuple((jax.ShapeDtypeStruct((SPAN...  68.6 us
    dot_general x15, matrix products, dot(): lax.dot_general(a, b, (((a_axis,), (b_axis,)), ((), ())), preferred_eleme...  19.7 us
    unnamed x66, local copies, waits for them, and re-layouts  5.71 us
  transfers between devices with their start and end apart: 4, of which 1 were waited for; matrix products, arithmetic and copies ran while one was open for 7% of the time, Pallas kernels for 37%

profile of v3, /device:TPU:0, one launch (start us, length us, event | category | flops | bytes accessed | tf_op | source)
XLA Modules:
  0.0 215.4 jit_solution(2506971701755237303)
XLA Ops:
  0.6 0.9 slice.81
  1.5 1.4 slice_bitcast_fusion.2.refs_1_
  4.1 1.3 reduce.49
  5.6 0.7 reshape.353
  6.3 1.0 convert_element_type.131
  7.3 0.9 concatenate.23
  8.8 68.6 %gather.1 = (bf16[16,48,768]{2,1,0:T(8,128)(2,1)}, bf16[16,48,384]{2,1,0:T(8,128)(2,1)}, bf16[16,48,1536]{2,1,0:T(8,128)(2,1)}, bf16[16,48,1536]{2,1,0:T(8,128)(...) custom-call(bf16[48,768]{1,0:T(8,128)(2,1)} %bitcast.173, bf16[48,384]{1,0:T(8,128)(2,1)} %slice_bitcast_fusion.2.refs_1_, ...), custom_call_target="tpu_custom_call" | custom-call | tf_op jit(solution)/shard_map/gather/pallas_call | solution.py:194
  77.4 0.9 slice_convert_fusion.1
  79.9 1.8 fusion.25
  82.5 1.1 fusion.27
  83.6 1.2 convolution_convert_fusion.7
  84.8 1.1 fusion.79
  85.9 0.9 slice.114
  86.8 0.8 slice_bitcast_fusion.1
  88.1 1.4 fusion.69
  89.7 1.5 multiply_convert_fusion
  91.2 0.7 copy-done.2
  91.9 1.6 fusion.80
  94.3 1.4 collective-permute-done.1
  95.7 1.3 fusion.68
  97.3 1.3 multiply_reduce_fusion.1
  98.6 1.0 fusion.66
  99.6 0.7 fusion.74
  100.3 1.6 fusion.30
  102.3 2.2 %convolution_convert_fusion = bf16[768,1536]{1,0:T(8,128)(2,1)} fusion(bf16[128,1536]{1,0:T(8,128)(2,1)S(1)} %copy-done.3, f32[128,768]{1,0:T(8,128)S(1)} %get-tuple-element.83), kind=kOutput, calls=%fused_computation.1 | convolution fusion | flops 303267840 | bytes 3145728 | tf_op jit(solution)/shard_map/dot_general | solution.py:429
  106.7 3.3 %convolution_convert_fusion.1 = bf16[768,1536]{1,0:T(8,128)(2,1)} fusion(bf16[128,1536]{1,0:T(8,128)(2,1)} %copy-done.16, f32[128,768]{1,0:T(8,128)S(1)} %get-tuple-element.90, f32[768]{0:T(1024)S(1)} %add.153, f32[768]{0:T(1024)S(1)} %mul.162, f32[128]{0:T(128)S(1)} %add_rsqrt_fusion.1, f32[128]{0:T(128)S(1)} %broadcast_multiply_fusion.5), kind=kOutput, calls=%fused_computation.2 | convolution fusion | flops 303661056 | bytes 3152896 | tf_op jit(solution)/shard_map/dot_general | solution.py:429
  110.0 1.9 multiply_reduce_fusion.2
  111.9 0.8 fusion.67
  113.5 0.9 fusion.71
  114.4 1.2 convolution_convert_fusion.3
  115.6 0.9 fusion.70
  116.5 1.6 fusion.7
  118.5 1.1 fusion.81
  119.5 0.8 stack.50
  120.3 0.8 stack.51
  121.2 0.8 stack.47
  122.0 0.8 stack.48
  122.8 0.9 pad_maximum_fusion.1
  123.8 1.5 convolution_convert_fusion.2
  125.3 1.1 copy.44
  127.2 0.7 fusion.51.refs_5_
  127.9 79.3 %scatter.1 = (f32[48,768]{1,0:T(8,128)}, f32[48,384]{1,0:T(8,128)}, f32[48,1536]{1,0:T(8,128)}, f32[48,1536]{1,0:T(8,128)}, f32[48,384]{1,0:T(8,128)}, /*index=5*/f32[16,128]{1,0:T(8,128)}) custom-call(bf16[16,48,768]{2,1,0:T(8,128)(2,1)} %bitcast.149, bf16[16,48,384]{2,1,0:T(8,128)(2,1)} %bitcast.153, bf16[16,48,1536]{2,1,0:T(8,128)(2,1)} %bitcast.146, ...), custom_call_target="tpu_custom_call" | custom-call | tf_op jit(solution)/shard_map/scatter/pallas_call | solution.py:376
  207.3 1.0 pad_maximum_fusion
  208.4 0.7 copy.53
  209.8 1.5 fusion.72
  212.5 0.8 add_bitcast_fusion
  214.0 0.7 copy.64
  214.7 0.7 copy.65
  (117 shorter events, 12.6 us)
Async XLA Ops:
  78.3 0.7 copy-start.21
  79.1 5.7 %copy-start.10 = (bf16[16,48,384]{2,1,0:T(8,128)(2,1)S(1)}, bf16[16,48,384]{2,1,0:T(8,128)(2,1)}, u32[]{:S(2)}) copy-start(bf16[16,48,384]{2,1,0:T(8,128)(2,1)} %get-tuple-element.29) | copy-start | bytes 1769476
  79.2 3.0 %copy-start.28 = (f32[6,64]{1,0:T(8,128)}, f32[6,64]{1,0:T(8,128)S(1)}, u32[]{:S(2)}) copy-start(f32[6,64]{1,0:T(8,128)S(1)} %add.143) | copy-start | bytes 4612
  79.2 3.3 %copy-start.8 = (bf16[16,48,384]{2,1,0:T(8,128)(2,1)S(1)}, bf16[16,48,384]{2,1,0:T(8,128)(2,1)}, u32[]{:S(2)}) copy-start(bf16[16,48,384]{2,1,0:T(8,128)(2,1)} %get-tuple-element.26) | copy-start | bytes 1769476
  81.7 0.8 copy-start.13
  82.5 7.2 %copy-start = (bf16[16,48,1536]{2,1,0:T(8,128)(2,1)S(1)}, bf16[16,48,1536]{2,1,0:T(8,128)(2,1)}, u32[]{:S(2)}) copy-start(bf16[16,48,1536]{2,1,0:T(8,128)(2,1)} %get-tuple-element.30) | copy-start | bytes 7077892
  84.8 1.1 copy-start.18
  85.9 2.2 %collective-permute-start = (f32[128,768]{1,0:T(8,128)}, f32[128,768]{1,0:T(8,128)}, u32[]{:S(2)}, u32[]{:S(2)}) collective-permute-start(f32[128,768]{1,0:T(8,128)} %fusion.79), channel_id=1, source_target_pairs={{0,1},{1,0},{2,3},{3,2},{4,5},{5,4},{6,7},{7,6},{8,9},{9,8},{10,11... | collective-permute-start | bytes 1179656 | tf_op jit(solution)/shard_map/ppermute | solution.py:423
  89.5 2.4 %copy-start.6 = (bf16[16,48,1536]{2,1,0:T(8,128)(2,1)S(1)}, bf16[16,48,1536]{2,1,0:T(8,128)(2,1)}, u32[]{:S(2)}) copy-start(bf16[16,48,1536]{2,1,0:T(8,128)(2,1)} %get-tuple-element.31) | copy-start | bytes 7077892
  91.2 0.7 copy-start.2
  93.5 2.2 %collective-permute-start.1 = (f32[128,768]{1,0:T(8,128)}, f32[128,768]{1,0:T(8,128)}, u32[]{:S(2)}, u32[]{:S(2)}) collective-permute-start(f32[128,768]{1,0:T(8,128)} %fusion.80), channel_id=1, source_target_pairs={{0,1},{1,0},{2,3},{3,2},{4,5},{5,4},{6,7},{7,6},{8,9},{9,8},{10,11... | collective-permute-start | bytes 1179656 | tf_op jit(solution)/shard_map/ppermute | solution.py:423
  94.3 4.3 %copy-start.15 = (f32[1,128,768]{2,1,0:T(8,128)S(1)}, f32[1,128,768]{2,1,0:T(8,128)}, u32[]{:S(2)}) copy-start(f32[1,128,768]{2,1,0:T(8,128)} %param.17) | copy-start | bytes 1179652
  94.3 5.3 %copy-start.7 = (bf16[16,48,1536]{2,1,0:T(8,128)(2,1)S(1)}, bf16[16,48,1536]{2,1,0:T(8,128)(2,1)}, u32[]{:S(2)}) copy-start(bf16[16,48,1536]{2,1,0:T(8,128)(2,1)} %get-tuple-element.31) | copy-start | bytes 7077892
  94.3 5.3 %copy-start.20 = (f32[128,1536]{1,0:T(8,128)S(1)}, f32[128,1536]{1,0:T(8,128)}, u32[]{:S(2)}) copy-start(f32[128,1536]{1,0:T(8,128)} %get-tuple-element.106) | copy-start | bytes 2359300
  99.6 2.7 %copy-start.4 = (f32[128,768]{1,0:T(8,128)}, f32[128,768]{1,0:T(8,128)S(1)}, u32[]{:S(2)}) copy-start(f32[128,768]{1,0:T(8,128)S(1)} %get-tuple-element.83) | copy-start | bytes 1179652
  100.3 4.2 %copy-start.16 = (bf16[128,1536]{1,0:T(8,128)(2,1)}, bf16[128,1536]{1,0:T(8,128)(2,1)S(1)}, u32[]{:S(2)}) copy-start(bf16[128,1536]{1,0:T(8,128)(2,1)S(1)} %get-tuple-element.109) | copy-start | bytes 1179652
  100.3 2.0 copy-start.3
  102.0 8.0 %collective-permute-start.2 = (f32[128,768]{1,0:T(8,128)}, f32[128,768]{1,0:T(8,128)S(1)}, u32[]{:S(2)}, u32[]{:S(2)}) collective-permute-start(f32[128,768]{1,0:T(8,128)} %fusion.30), channel_id=1, source_target_pairs={{0,1},{1,0},{2,3},{3,2},{4,5},{5,4},{6,7},{7,6},{8,9},{9,8},{10,11... | collective-permute-start | bytes 1179656 | tf_op jit(solution)/shard_map/ppermute | solution.py:423
  104.6 5.4 %copy-start.5 = (f32[128,768]{1,0:T(8,128)S(1)}, f32[128,768]{1,0:T(8,128)}, u32[]{:S(2)}) copy-start(f32[128,768]{1,0:T(8,128)} %copy-done.4) | copy-start | bytes 1179652
  110.0 2.7 %copy-start.11 = (bf16[16,48,384]{2,1,0:T(8,128)(2,1)S(1)}, bf16[16,48,384]{2,1,0:T(8,128)(2,1)}, u32[]{:S(2)}) copy-start(bf16[16,48,384]{2,1,0:T(8,128)(2,1)} %get-tuple-element.29) | copy-start | bytes 1769476
  110.0 3.1 %copy-start.12 = (f32[384,128]{1,0:T(8,128)S(1)}, f32[384,128]{1,0:T(8,128)}, u32[]{:S(2)}) copy-start(f32[384,128]{1,0:T(8,128)} %fusion.27) | copy-start | bytes 589828
  111.9 2.5 %copy-start.19 = (bf16[6,64,128]{2,1,0:T(8,128)(2,1)S(1)}, bf16[6,64,128]{2,1,0:T(8,128)(2,1)}, u32[]{:S(2)}) copy-start(bf16[6,64,128]{2,1,0:T(8,128)(2,1)} %copy-done.18) | copy-start | bytes 294916
  111.9 3.7 %copy-start.14 = (f32[768,128]{1,0:T(8,128)S(1)}, f32[768,128]{1,0:T(8,128)}, u32[]{:S(2)}) copy-start(f32[768,128]{1,0:T(8,128)} %copy-done.13) | copy-start | bytes 1179652
  113.1 5.4 %copy-start.9 = (bf16[16,48,384]{2,1,0:T(8,128)(2,1)S(1)}, bf16[16,48,384]{2,1,0:T(8,128)(2,1)}, u32[]{:S(2)}) copy-start(bf16[16,48,384]{2,1,0:T(8,128)(2,1)} %get-tuple-element.26) | copy-start | bytes 1769476
  114.4 6.7 %copy-start.29 = (bf16[768]{0:T(1024)(128)(2,1)S(1)}, bf16[768]{0:T(1024)(128)(2,1)}, u32[]{:S(2)}) copy-start(bf16[768]{0:T(1024)(128)(2,1)} %get-tuple-element.73) | copy-start | bytes 4612
  118.4 7.9 %copy-start.1 = (bf16[16,48,768]{2,1,0:T(8,128)(2,1)S(1)}, bf16[16,48,768]{2,1,0:T(8,128)(2,1)}, u32[]{:S(2)}) copy-start(bf16[16,48,768]{2,1,0:T(8,128)(2,1)} %get-tuple-element.28) | copy-start | bytes 3538948
  119.5 6.8 %copy-start.17 = (f32[128,768]{1,0:T(8,128)S(1)}, f32[128,768]{1,0:T(8,128)}, u32[]{:S(2)}) copy-start(f32[128,768]{1,0:T(8,128)} %fusion.81) | copy-start | bytes 1179652
  123.8 3.4 %copy-start.25 = (bf16[1,16,48]{2,0,1:T(2,128)(2,1)S(1)}, bf16[1,16,48]{2,0,1:T(2,128)(2,1)}, u32[]{:S(2)}) copy-start(bf16[1,16,48]{2,0,1:T(2,128)(2,1)} %stack.53) | copy-start | bytes 4612
  123.8 3.3 %copy-start.26 = (bf16[1,16,48]{2,0,1:T(2,128)(2,1)S(1)}, bf16[1,16,48]{2,0,1:T(2,128)(2,1)}, u32[]{:S(2)}) copy-start(bf16[1,16,48]{2,0,1:T(2,128)(2,1)} %stack.54) | copy-start | bytes 4612
  123.8 3.3 %copy-start.27 = (bf16[1,16,48]{2,0,1:T(2,128)(2,1)S(1)}, bf16[1,16,48]{2,0,1:T(2,128)(2,1)}, u32[]{:S(2)}) copy-start(bf16[1,16,48]{2,0,1:T(2,128)(2,1)} %stack.55) | copy-start | bytes 4612
  126.9 85.6 %collective-permute-start.3 = (f32[128,768]{1,0:T(8,128)S(1)}, f32[128,768]{1,0:T(8,128)S(1)}, u32[]{:S(2)}, u32[]{:S(2)}) collective-permute-start(f32[128,768]{1,0:T(8,128)S(1)} %convolution_add_fusion.1), channel_id=1, source_target_pairs={{0,1},{1,0},{2,3},{3,2},{4,5},{5,4},{6,7},{7,6},{8,9},{9,8},{10,11... | collective-permute-start | bytes 1179656 | tf_op jit(solution)/shard_map/ppermute | solution.py:423
  207.2 6.1 %copy-start.24 = (f32[48,384]{1,0:T(8,128)S(1)}, f32[48,384]{1,0:T(8,128)}, u32[]{:S(2)}) copy-start(f32[48,384]{1,0:T(8,128)} %get-tuple-element.35) | copy-start | bytes 221188
  207.3 6.7 %copy-start.23 = (f32[48,1536]{1,0:T(8,128)S(1)}, f32[48,1536]{1,0:T(8,128)}, u32[]{:S(2)}) copy-start(f32[48,1536]{1,0:T(8,128)} %get-tuple-element.36) | copy-start | bytes 884740
  207.3 7.4 %copy-start.22 = (f32[48,1536]{1,0:T(8,128)S(1)}, f32[48,1536]{1,0:T(8,128)}, u32[]{:S(2)}) copy-start(f32[48,1536]{1,0:T(8,128)} %get-tuple-element.37) | copy-start | bytes 884740
